TPU v7x, 256 devices: a whole 4x4x8 slice. The times are simulated.
256 devices in a mesh: grp: 8 (over y, core), dp: 32 (over z, x).
Axes of the slice: x: 4, y: 4, z: 8, core: 2. Of those that a mesh axis runs over, the one named last changes fastest.
Arguments:
- query: bfloat16 [4096, 64, 576], P(('grp', 'dp')), parts along dimension 0, may hold values from -34 to 34
- cache: bfloat16 [4096, 256, 576], P(('grp', 'dp')), parts along dimension 0, may hold values from -6 to 6
- new_latent: bfloat16 [4096, 576], P(('grp', 'dp')), parts along dimension 0, may hold values from -6 to 6
- lengths: int32 [4096], P(('grp', 'dp')), parts along dimension 0, may hold values from 64 to 256, as said below
- counts: int32 [256], P(('grp', 'dp')), parts along dimension 0, may hold values from 8 to 16, as said below
- hidden_in: bfloat16 [4096, 3584], P(('grp', 'dp')), parts along dimension 0, may hold values from -6 to 6
- value_up: bfloat16 [64, 512, 128], P('dp'), may hold values from -0.75 to 0.75
- out_proj: bfloat16 [8192, 3584], P('dp'), may hold values from -0.0625 to 0.0625
- norm_gain: bfloat16 [3584], replicated, may hold values from 0.099609375 to 1.8984375
- w_gate: bfloat16 [3584, 9216], P(None, 'dp'), may hold values from -0.09375 to 0.09375
- w_up: bfloat16 [3584, 9216], P(None, 'dp'), may hold values from -0.09375 to 0.09375
- w_down: bfloat16 [9216, 3584], P('dp'), may hold values from -0.125 to 0.125
Outputs:
- mixed: bfloat16 [4096, 3584], P(('grp', 'dp')), parts along dimension 0
There are 8 independent parts, one for each index of `grp`. A program takes and returns all parts, laid end to end along the dimension named above; an argument that names none is the same for every part. Nothing has to cross between parts.
Inputs may be any that keep to these rules, and one draw needn't show every extreme that they name: `lengths`: device d holds requests d * 16 to (d + 1) * 16 - 1; some request has exactly 256 cached positions. Slots 0 to counts[d] - 1 of device d are live; some device is full.
All inputs are finite; a program needn't handle non-finite values.
Results may differ from a plain program's by a relative error of at most 0.03.
Values may be sent and summed in bfloat16 or wider, within the bound.
A program may use at most 128 MiB of HBM per device.

v0:
```python
import jax
import jax.numpy as jnp
from jax import lax
from jax.sharding import PartitionSpec as P

score_scale = 192.0 ** (-0.5)


def rms_rows(residual, norm_gain):
    mean_sq = jnp.mean(residual * residual, axis=-1, keepdims=True)
    return (residual * lax.rsqrt(mean_sq + 1e-06) * norm_gain.astype(jnp.float32)).astype(
        jnp.bfloat16
    )


def per_device(
    query,
    cache,
    new_latent,
    lengths,
    counts,
    hidden_in,
    value_up,
    out_proj,
    norm_gain,
    w_gate,
    w_up,
    w_down,
):
    slot_count = query.shape[0]
    latent_width = value_up.shape[1]
    scores = (
        jnp.einsum("rhk,rck->rhc", query, cache, preferred_element_type=jnp.float32) * score_scale
    )
    self_score = (
        jnp.einsum("rhk,rk->rh", query, new_latent, preferred_element_type=jnp.float32)
        * score_scale
    )
    positions = jnp.arange(cache.shape[1], dtype=jnp.int32)
    in_range = positions[None, None, :] < lengths[:, None, None]
    scores = jnp.where(in_range, scores, -jnp.inf)
    row_max = jnp.maximum(jnp.max(scores, axis=-1), self_score)
    weights = jnp.exp(scores - row_max[..., None])
    self_weight = jnp.exp(self_score - row_max)
    denom_sum = jnp.sum(weights, axis=-1) + self_weight
    weights_b = weights.astype(jnp.bfloat16)
    self_b = self_weight.astype(jnp.bfloat16).astype(jnp.float32)
    mixed_sum = jnp.einsum(
        "rhc,rcl->rhl", weights_b, cache[:, :, :latent_width], preferred_element_type=jnp.float32
    )
    mixed_sum = mixed_sum + self_b[..., None] * new_latent[:, None, :latent_width].astype(
        jnp.float32
    )
    latent_out = (mixed_sum / denom_sum[..., None]).astype(jnp.bfloat16)
    exchanged = lax.all_to_all(latent_out, "dp", split_axis=1, concat_axis=0, tiled=True)
    heads_out = jnp.einsum(
        "rhl,hlv->rhv", exchanged, value_up, preferred_element_type=jnp.float32
    ).astype(jnp.bfloat16)
    flat_heads = heads_out.reshape(heads_out.shape[0], -1)
    picked = flat_heads
    residual = lax.psum_scatter(
        jnp.dot(picked, out_proj, preferred_element_type=jnp.float32).astype(jnp.bfloat16),
        "dp",
        scatter_dimension=0,
        tiled=True,
    ).astype(jnp.float32) + hidden_in.astype(jnp.float32)
    normed = rms_rows(residual, norm_gain)
    piece_rows = lax.all_gather(normed, "dp", axis=0, tiled=True)
    gate_act = jnp.dot(piece_rows, w_gate, preferred_element_type=jnp.float32)
    up_act = jnp.dot(piece_rows, w_up, preferred_element_type=jnp.float32)
    inner_act = (jax.nn.silu(gate_act) * up_act).astype(jnp.bfloat16)
    picked = inner_act
    ffn_out = lax.psum_scatter(
        jnp.dot(picked, w_down, preferred_element_type=jnp.float32).astype(jnp.bfloat16),
        "dp",
        scatter_dimension=0,
        tiled=True,
    ).astype(jnp.float32)
    live_rows = jnp.arange(slot_count, dtype=jnp.int32) < counts[0]
    return jnp.where(live_rows[:, None], residual + ffn_out, 0.0).astype(jnp.bfloat16)


def solution(mesh):
    return jax.shard_map(
        per_device,
        mesh=mesh,
        in_specs=(
            P(("grp", "dp"), None, None),
            P(("grp", "dp"), None, None),
            P(("grp", "dp"), None),
            P(("grp", "dp")),
            P(("grp", "dp")),
            P(("grp", "dp"), None),
            P("dp", None, None),
            P("dp", None),
            P(),
            P(None, "dp"),
            P(None, "dp"),
            P("dp", None),
        ),
        out_specs=P(("grp", "dp"), None),
        check_vma=False,
    )
```

profile of v0, /device:TPU:8, one launch (start us, length us, event | category | flops | bytes accessed | tf_op | source)
XLA Modules:
  0.0 595.9 jit_solution(10815839318144002262)
XLA Ops:
  6.5 0.0 copy-start
  6.5 0.0 copy-start.2
  6.5 0.0 reduce-scatter.3.cloned.1.call-start
  6.5 0.9 iota_compare_fusion
  7.4 0.8 slice_convert_fusion
  8.2 0.0 slice-start
  8.2 2.0 fusion.16
  10.2 0.0 copy-done.2
  10.2 0.0 slice-start.1
  10.2 3.5 fusion.20
  13.7 0.4 fusion.6
  14.1 0.0 slice-done
  14.1 0.0 slice-done.1
  14.1 1.6 divide_convert_fusion
  15.7 0.6 copy.17
  16.3 0.0 copy-start.5
  16.3 39.3 %all_to_all.18 = bf16[16,64,512]{2,0,1:T(8,128)(2,1)S(1)} all-to-all(bf16[16,64,512]{2,0,1:T(8,128)(2,1)S(1)} %copy.17), channel_id=1, replica_groups=mesh['grp'=8,'dp'=32] {'dp'}, dimensions={1} | all-to-all | bytes 2097152 | tf_op jit(solution)/shard_map/all_to_all | solution.py:55
  55.6 0.0 copy-start.1
  55.6 0.1 copy.18
  55.7 0.0 copy-done.5
  55.7 0.5 convolution_convert_fusion.2
  56.2 0.9 copy-done.1
  57.1 2.9 convolution_convert_fusion.1
  60.1 0.0 copy-start.6
  60.1 0.0 copy-start.3
  60.1 0.0 reduce-scatter.3.cloned.1.call-update
  60.1 0.0 all-gather.2.cloned.1.call-start
  60.1 0.6 copy-done.6
  60.8 216.2 %reduce-scatter.3.cloned.1.call-done = bf16[16,3584]{1,0:T(8,128)(2,1)} async-done(((bf16[512,3584]{1,0:T(8,128)(2,1)}), bf16[16,3584]{1,0:T(8,128)(2,1)}) %reduce-scatter.3.cloned.1.call-update) | async-done | bytes 114704 | tf_op jit(solution)/shard_map/reduce_scatter | solution.py:61
  276.9 0.0 copy-done.3
  276.9 1.0 multiply_reduce_fusion
  278.0 1.6 multiply_convert_fusion
  279.6 0.0 all-gather.2.cloned.1.call-update
  279.6 0.0 reduce-scatter.5.cloned.1.call-start
  279.7 79.3 %all-gather.2.cloned.1.call-done = bf16[512,3584]{1,0:T(8,128)(2,1)} async-done(((bf16[16,3584]{1,0:T(8,128)(2,1)}), bf16[512,3584]{1,0:T(8,128)(2,1)}) %all-gather.2.cloned.1.call-update) | async-done | bytes 3670032 | tf_op jit(solution)/shard_map/all_gather | solution.py:68
  358.9 3.9 fusion.21
  362.9 0.0 copy-done
  362.9 7.8 %convolution_convert_fusion = bf16[512,3584]{1,0:T(8,128)(2,1)} fusion(bf16[288,3584]{1,0:T(8,128)(2,1)S(1)} %copy-done, bf16[512,3584]{1,0:T(8,128)(2,1)} %all-gather.2.cloned.1.call-done, bf16[3584,288]{0,1:T(8,128)(2,1)} %param.22, f32[512,288]{0,1:T(8,128)S(1)} %fusion.21), kind=kOutput, calls=%fused_computation | convolution fusion | flops 2116648960 | bytes 12058624 | tf_op jit(solution)/shard_map/dot_general | solution.py:74
  370.7 0.0 copy-start.4
  370.7 0.0 reduce-scatter.5.cloned.1.call-update
  371.5 216.2 %reduce-scatter.5.cloned.1.call-done = bf16[16,3584]{1,0:T(8,128)(2,1)} async-done(((bf16[512,3584]{1,0:T(8,128)(2,1)}), bf16[16,3584]{1,0:T(8,128)(2,1)}) %reduce-scatter.5.cloned.1.call-update) | async-done | bytes 114704 | tf_op jit(solution)/shard_map/reduce_scatter | solution.py:73
  587.7 0.0 copy-done.4
  587.7 1.6 select_convert_fusion
  (6 shorter events, 0.0 us)
Async XLA Ops:
  6.5 356.4 %copy-start = (bf16[288,3584]{1,0:T(8,128)(2,1)S(1)}, bf16[288,3584]{1,0:T(8,128)(2,1)}, u32[]{:S(2)}) copy-start(bf16[288,3584]{1,0:T(8,128)(2,1)} %param.23) | copy-start | bytes 6193156
  6.5 3.6 copy-start.2
  6.5 270.4 %reduce-scatter.3.cloned.1.call-start = ((), (), s32[]{:S(2)}) async-start(), calls=%async_computation.3 | async-start | bytes 3784704 | tf_op jit(solution)/shard_map/reduce_scatter | solution.py:61
  8.2 5.9 slice-start
  10.2 3.9 slice-start.1
  16.3 39.4 %copy-start.5 = (bf16[2,512,128]{2,1,0:T(8,128)(2,1)S(1)}, bf16[2,512,128]{2,1,0:T(8,128)(2,1)}, u32[]{:S(2)}) copy-start(bf16[2,512,128]{2,1,0:T(8,128)(2,1)} %param.18) | copy-start | bytes 786436
  55.6 1.5 copy-start.1
  60.1 0.7 copy-start.6
  60.1 216.9 %copy-start.3 = (bf16[16,3584]{1,0:T(8,128)(2,1)S(1)}, bf16[16,3584]{1,0:T(8,128)(2,1)}, u32[]{:S(2)}) copy-start(bf16[16,3584]{1,0:T(8,128)(2,1)} %param.17) | copy-start | bytes 344068
  60.1 298.9 %all-gather.2.cloned.1.call-start = ((), (), s32[]{:S(2)}) async-start(), calls=%async_computation.4 | async-start | bytes 3784704 | tf_op jit(solution)/shard_map/all_gather | solution.py:68
  279.6 308.1 %reduce-scatter.5.cloned.1.call-start = ((), (), s32[]{:S(2)}) async-start(), calls=%async_computation.5 | async-start | bytes 3784704 | tf_op jit(solution)/shard_map/reduce_scatter | solution.py:73
  370.7 217.0 %copy-start.4 = (bf16[16,3584]{1,0:T(8,128)(2,1)S(1)}, bf16[16,3584]{1,0:T(8,128)(2,1)}, u32[]{:S(2)}) copy-start(bf16[16,3584]{1,0:T(8,128)(2,1)} %reduce-scatter.3.cloned.1.call-done) | copy-start | bytes 344068
Sparse Core Ops, SparseCore 0:
  60.2 216.6 reduce-scatter.2
  279.8 79.0 all-gather.1
  370.9 216.7 reduce-scatter.4
where the time goes:
time: 596 us
  waiting for transfers between devices  512 us (86%)
  blocking collectives  39.3 us (7%)
  matrix products  22.2 us (4%)
  between operations  13.9 us (2%)
  other arithmetic  6.4 us (1%)
    reduce_scatter x1, waiting for transfers between devices, per_device(): lax.psum_scatter(jnp.dot(picked, w_down, preferred_element_type=jnp.float...  216 us
    reduce_scatter x1, waiting for transfers between devices, per_device(): lax.psum_scatter(jnp.dot(picked, out_proj, preferred_element_type=jnp.flo...  216 us
    all_gather x1, waiting for transfers between devices, per_device(): piece_rows = lax.all_gather(normed, 'dp', axis=0, tiled=True)  79.3 us
    all_to_all x1, blocking collectives, per_device(): lax.all_to_all(latent_out, 'dp', split_axis=1, concat_axis=0, tiled=True)  39.3 us
  transfers between devices with their start and end apart: 3, of which 3 were waited for; matrix products, arithmetic and copies ran while one was open for 0% of the time, Pallas kernels for 0%

commit v1 on v0

v1 whole, which is shorter than its diff:
```python
import jax
import jax.numpy as jnp
from jax import lax
from jax.experimental import pallas as pl
from jax.experimental.pallas import tpu as pltpu
from jax.sharding import PartitionSpec as P

score_scale = 192.0 ** (-0.5)
MESH = pl.DeviceIdType.MESH
F32 = jnp.float32
BF16 = jnp.bfloat16

NZ, NX = 8, 4
RB = 16
D = 3584
CA = 1792
CB = D - CA
HA, HB = CA // 2, CB // 2
PLUS, MINUS = 0, 1
RS_ORDER = (4, -3, 3, -2, 2, -1, 1, 0)


def acols(h):
    return slice(h * HA, (h + 1) * HA)


def bcols(h):
    return slice(CA + h * HB, CA + (h + 1) * HB)


class Net:
    def __init__(self):
        self.g = lax.axis_index("grp")
        d = lax.axis_index("dp")
        self.z = d // NX
        self.x = lax.rem(d, NX)

    def zc(self, k):
        return lax.rem(self.z + (k + NZ), NZ)

    def xc(self, k):
        return lax.rem(self.x + (k + NX), NX)

    def zdev(self, k):
        return (self.g, self.zc(k) * NX + self.x)

    def xdev(self, k):
        return (self.g, self.z * NX + self.xc(k))


class Sender:
    def __init__(self):
        self.started = []

    def start(self, src, dst, ssem, rsem, dev):
        copy = pltpu.make_async_remote_copy(
            src_ref=src,
            dst_ref=dst,
            send_sem=ssem,
            recv_sem=rsem,
            device_id=dev,
            device_id_type=MESH,
        )
        copy.start()
        self.started.append(copy)

    def finish(self):
        for copy in self.started:
            copy.wait_send()


def wait_recv(dst, ssem, rsem, dev):
    pltpu.make_async_remote_copy(
        src_ref=dst,
        dst_ref=dst,
        send_sem=ssem,
        recv_sem=rsem,
        device_id=dev,
        device_id_type=MESH,
    ).wait_recv()


RS_SCRATCH = [
    pltpu.VMEM((NZ, NX, RB, D), BF16),
    pltpu.VMEM((3, NZ, RB, CA), BF16),
    pltpu.VMEM((2, 4, 2, RB, HA), BF16),
    pltpu.VMEM((2, 4, 2, NX, RB, HB), BF16),
    pltpu.VMEM((3, RB, CB), BF16),
    pltpu.SemaphoreType.DMA((2, 3, NZ)),
    pltpu.SemaphoreType.DMA((2, 2, 4, 2)),
    pltpu.SemaphoreType.DMA((2, 2, 4, 2)),
    pltpu.SemaphoreType.DMA((2, 3)),
]
N_RS = len(RS_SCRATCH)


def reduce_scatter(net, send, make_part, total, scratch):
    part, ax, az, bz, bx, ax_sem, az_sem, bz_sem, bx_sem = scratch
    z, x = net.z, net.x

    def along_z(k, h, src, buf, sem, add):
        if k == 4:
            d = PLUS if h == 0 else MINUS
            hops = 4
        else:
            d = PLUS if k > 0 else MINUS
            hops = abs(k)
            if hops < 3 or h == d:
                slot = buf.at[d, hops, h]
                wait_recv(slot, sem.at[0, d, hops, h], sem.at[1, d, hops, h], net.zdev(0))
                add(slot)
            else:
                add(None)
        send.start(
            src,
            buf.at[d, hops - 1, h],
            sem.at[0, d, hops - 1, h],
            sem.at[1, d, hops - 1, h],
            net.zdev(1 if d == PLUS else -1),
        )

    def last_z(h, buf, sem):
        for d in (PLUS, MINUS):
            wait_recv(buf.at[d, 0, h], sem.at[0, d, 0, h], sem.at[1, d, 0, h], net.zdev(0))
        return buf[PLUS, 0, h].astype(F32) + buf[MINUS, 0, h].astype(F32)

    def first(i):
        k = RS_ORDER[i]
        c = net.zc(k)
        make_part(c, part)
        for h in range(2):
            cols = bcols(h)
            if k == 0:
                part[c, :, :, cols] = (part[c, :, :, cols].astype(F32) + last_z(h, bz, bz_sem)).astype(BF16)
                continue

            def add(slot):
                if slot is not None:
                    part[c, :, :, cols] = (
                        part[c, :, :, cols].astype(F32) + slot[...].astype(F32)
                    ).astype(BF16)

            along_z(k, h, part.at[c, :, :, cols], bz, bz_sem, add)
        for o in (1, 3, 2):
            send.start(
                part.at[c, net.xc(o), :, 0:CA],
                ax.at[o - 1, i],
                ax_sem.at[0, o - 1, i],
                ax_sem.at[1, o - 1, i],
                net.xdev(o),
            )
        if k == 0:
            for o in (1, 3, 2):
                send.start(
                    part.at[c, net.xc(o), :, CA:D],
                    bx.at[o - 1],
                    bx_sem.at[0, o - 1],
                    bx_sem.at[1, o - 1],
                    net.xdev(o),
                )

    def second(i):
        k = RS_ORDER[i]
        c = net.zc(k)
        for o in (1, 3, 2):
            wait_recv(ax.at[o - 1, i], ax_sem.at[0, o - 1, i], ax_sem.at[1, o - 1, i], net.zdev(0))
        for h in range(2):
            cols = acols(h)
            acc = part[c, x, :, cols].astype(F32)
            for o in range(3):
                acc = acc + ax[o, i, :, cols].astype(F32)
            if k == 0:
                total[:, cols] += acc + last_z(h, az, az_sem)
                continue

            def add(slot):
                value = acc if slot is None else acc + slot[...].astype(F32)
                part[c, x, :, cols] = value.astype(BF16)

            if k == 4:
                add(None)
            along_z(k, h, part.at[c, x, :, cols], az, az_sem, add)

    for i in range(NZ):
        first(i)
        if i:
            second(i - 1)
    second(NZ - 1)
    for o in (1, 3, 2):
        wait_recv(bx.at[o - 1], bx_sem.at[0, o - 1], bx_sem.at[1, o - 1], net.zdev(0))
    acc = part[z, x, :, CA:D].astype(F32)
    for o in range(3):
        acc = acc + bx[o].astype(F32)
    total[:, CA:D] += acc


AG_SCRATCH = [
    pltpu.VMEM((NZ, NX, RB, D), BF16),
    pltpu.SemaphoreType.DMA((2, 3, NZ)),
    pltpu.SemaphoreType.DMA((2, 2, 4)),
    pltpu.SemaphoreType.DMA((2, 2, 4, 2)),
    pltpu.SemaphoreType.DMA((2, 3)),
]
N_AG = len(AG_SCRATCH)


def all_gather(net, send, use, scratch):
    rows, ax_sem, az_sem, bz_sem, bx_sem = scratch
    z, x = net.z, net.x
    step = (1, -1)

    def to_x(i, k):
        c = net.zc(k)
        for o in (1, 3, 2):
            ref = rows.at[c, x, :, 0:CA]
            send.start(ref, ref, ax_sem.at[0, o - 1, i], ax_sem.at[1, o - 1, i], net.xdev(o))

    def from_x(i, k):
        c = net.zc(k)
        for o in (1, 3, 2):
            ref = rows.at[c, net.xc(-o), :, 0:CA]
            wait_recv(ref, ax_sem.at[0, o - 1, i], ax_sem.at[1, o - 1, i], net.zdev(0))

    def a_ref(k, hops, d):
        cols = slice(0, CA) if hops < 4 else acols(d)
        return rows.at[net.zc(k), x, :, cols]

    def a_send(hops, d):
        ref = a_ref(-step[d] * (hops - 1), hops, d)
        sems = az_sem.at[0, d, hops - 1], az_sem.at[1, d, hops - 1]
        send.start(ref, ref, *sems, net.zdev(step[d]))

    def a_wait(hops, d):
        ref = a_ref(-step[d] * hops, hops, d)
        wait_recv(ref, az_sem.at[0, d, hops - 1], az_sem.at[1, d, hops - 1], net.zdev(0))

    def b_send(hops, d, h):
        ref = rows.at[net.zc(-step[d] * (hops - 1)), :, :, bcols(h)]
        sems = bz_sem.at[0, d, hops - 1, h], bz_sem.at[1, d, hops - 1, h]
        send.start(ref, ref, *sems, net.zdev(step[d]))

    def b_wait(hops, d, h):
        ref = rows.at[net.zc(-step[d] * hops), :, :, bcols(h)]
        sems = bz_sem.at[0, d, hops - 1, h], bz_sem.at[1, d, hops - 1, h]
        wait_recv(ref, *sems, net.zdev(0))

    own_b = rows.at[z, x, :, CA:D]
    for o in (1, 3, 2):
        send.start(own_b, own_b, bx_sem.at[0, o - 1], bx_sem.at[1, o - 1], net.xdev(o))
    for d in (PLUS, MINUS):
        a_send(1, d)
    to_x(0, 0)
    for o in (1, 3, 2):
        ref = rows.at[z, net.xc(-o), :, CA:D]
        wait_recv(ref, bx_sem.at[0, o - 1], bx_sem.at[1, o - 1], net.zdev(0))
    for h in range(2):
        for d in (PLUS, MINUS):
            b_send(1, d, h if d == PLUS else 1 - h)
    pending = [(0, 0)]

    def use_next():
        i, k = pending.pop(0)
        from_x(i, k)
        use(net.zc(k))

    i = 1
    for hops in range(1, 4):
        for d in (PLUS, MINUS):
            k = -step[d] * hops
            a_wait(hops, d)
            a_send(hops + 1, d)
            to_x(i, k)
            for h in (d, 1 - d):
                b_wait(hops, d, h)
                if hops < 3 or h == d:
                    b_send(hops + 1, d, h)
            use_next()
            pending.append((i, k))
            i += 1
    for d in (PLUS, MINUS):
        a_wait(4, d)
    to_x(i, 4)
    pending.append((i, 4))
    use_next()
    for d in (PLUS, MINUS):
        b_wait(4, d, d)
    while pending:
        use_next()


def block_kernel(
    heads,
    hidden,
    gain,
    counts,
    wo_hbm,
    wg_hbm,
    wu_hbm,
    wd_hbm,
    out,
    wo,
    wg,
    wu,
    wd,
    w_sem,
    inner,
    total,
    ffn,
    *scratch,
):
    rs1, rs2, ag = scratch[:N_RS], scratch[N_RS : 2 * N_RS], scratch[2 * N_RS :]
    net = Net()
    send = Sender()
    weights = [
        pltpu.make_async_copy(src, dst, w_sem.at[i])
        for i, (src, dst) in enumerate(((wo_hbm, wo), (wg_hbm, wg), (wu_hbm, wu), (wd_hbm, wd)))
    ]
    for copy in weights:
        copy.start()
    barrier = pltpu.get_barrier_semaphore()
    partners = [net.zdev(1), net.zdev(-1)] + [net.xdev(o) for o in (1, 2, 3)]
    for dev in partners:
        pl.semaphore_signal(barrier, inc=1, device_id=dev, device_id_type=MESH)
    pl.semaphore_wait(barrier, len(partners))

    weights[0].wait()

    def project(c, part):
        value = jnp.dot(heads[c], wo[...], preferred_element_type=F32)
        part[c] = value.astype(BF16).reshape(NX, RB, D)

    total[...] = hidden[...].astype(F32)
    reduce_scatter(net, send, project, total, rs1)

    rows = ag[0]
    residual = total[...]
    mean_sq = jnp.mean(residual * residual, axis=-1, keepdims=True)
    rows[net.z, net.x] = (residual * lax.rsqrt(mean_sq + 1e-06) * gain[...].astype(F32)).astype(BF16)

    weights[1].wait()
    weights[2].wait()

    def feed(c):
        chunk = rows[c].reshape(NX * RB, D)
        gate = jnp.dot(chunk, wg[...], preferred_element_type=F32)
        up = jnp.dot(chunk, wu[...], preferred_element_type=F32)
        inner[c] = (gate / (1.0 + jnp.exp(-gate)) * up).astype(BF16)

    all_gather(net, send, feed, ag)

    weights[3].wait()

    def down(c, part):
        value = jnp.dot(inner[c], wd[...], preferred_element_type=F32)
        part[c] = value.astype(BF16).reshape(NX, RB, D)

    ffn[...] = total[...]
    reduce_scatter(net, send, down, ffn, rs2)
    live = lax.broadcasted_iota(jnp.int32, (RB, D), 0) < counts[0]
    out[...] = jnp.where(live, ffn[...], 0.0).astype(BF16)
    send.finish()


def block(heads, hidden, gain, counts, wo, wg, wu, wd):
    vmem = pl.BlockSpec(memory_space=pltpu.VMEM)
    hbm = pl.BlockSpec(memory_space=pl.ANY)
    n_inner = wg.shape[1]
    return pl.pallas_call(
        block_kernel,
        out_shape=jax.ShapeDtypeStruct((RB, D), BF16),
        in_specs=[vmem, vmem, vmem, pl.BlockSpec(memory_space=pltpu.SMEM), hbm, hbm, hbm, hbm],
        out_specs=vmem,
        scratch_shapes=[
            pltpu.VMEM(wo.shape, BF16),
            pltpu.VMEM(wg.shape, BF16),
            pltpu.VMEM(wu.shape, BF16),
            pltpu.VMEM(wd.shape, BF16),
            pltpu.SemaphoreType.DMA((4,)),
            pltpu.VMEM((NZ, NX * RB, n_inner), BF16),
            pltpu.VMEM((RB, D), F32),
            pltpu.VMEM((RB, D), F32),
            *RS_SCRATCH,
            *RS_SCRATCH,
            *AG_SCRATCH,
        ],
        compiler_params=pltpu.CompilerParams(
            collective_id=1, has_side_effects=True, vmem_limit_bytes=56 << 20
        ),
        name="block",
    )(heads, hidden, gain, counts, wo, wg, wu, wd)


def per_device(
    query,
    cache,
    new_latent,
    lengths,
    counts,
    hidden_in,
    value_up,
    out_proj,
    norm_gain,
    w_gate,
    w_up,
    w_down,
):
    latent_width = value_up.shape[1]
    scores = (
        jnp.einsum("rhk,rck->rhc", query, cache, preferred_element_type=jnp.float32) * score_scale
    )
    self_score = (
        jnp.einsum("rhk,rk->rh", query, new_latent, preferred_element_type=jnp.float32)
        * score_scale
    )
    positions = jnp.arange(cache.shape[1], dtype=jnp.int32)
    in_range = positions[None, None, :] < lengths[:, None, None]
    scores = jnp.where(in_range, scores, -jnp.inf)
    row_max = jnp.maximum(jnp.max(scores, axis=-1), self_score)
    weights = jnp.exp(scores - row_max[..., None])
    self_weight = jnp.exp(self_score - row_max)
    denom_sum = jnp.sum(weights, axis=-1) + self_weight
    weights_b = weights.astype(jnp.bfloat16)
    self_b = self_weight.astype(jnp.bfloat16).astype(jnp.float32)
    mixed_sum = jnp.einsum(
        "rhc,rcl->rhl", weights_b, cache[:, :, :latent_width], preferred_element_type=jnp.float32
    )
    mixed_sum = mixed_sum + self_b[..., None] * new_latent[:, None, :latent_width].astype(
        jnp.float32
    )
    latent_out = (mixed_sum / denom_sum[..., None]).astype(jnp.bfloat16)
    exchanged = lax.all_to_all(latent_out, "dp", split_axis=1, concat_axis=0, tiled=True)
    heads_out = jnp.einsum(
        "rhl,hlv->rhv", exchanged, value_up, preferred_element_type=jnp.float32
    ).astype(jnp.bfloat16)
    heads = heads_out.reshape(NZ, NX * RB, -1)
    return block(
        heads, hidden_in, norm_gain.reshape(1, D), counts, out_proj, w_gate, w_up, w_down
    )


def solution(mesh):
    return jax.shard_map(
        per_device,
        mesh=mesh,
        in_specs=(
            P(("grp", "dp"), None, None),
            P(("grp", "dp"), None, None),
            P(("grp", "dp"), None),
            P(("grp", "dp")),
            P(("grp", "dp")),
            P(("grp", "dp"), None),
            P("dp", None, None),
            P("dp", None),
            P(),
            P(None, "dp"),
            P(None, "dp"),
            P("dp", None),
        ),
        out_specs=P(("grp", "dp"), None),
        check_vma=False,
    )
```

time: 596 us -> 162 us (0.27)
  waiting for transfers between devices: 512 us -> 18.1 us
  Pallas kernels: 0 us -> 109 us
  blocking collectives: 39.3 us -> 0 us
  matrix products: 22.2 us -> 6.86 us
  between operations: 13.9 us -> 0.78 us
  local copies, waits for them, and re-layouts: 2.22 us -> 13.7 us
  starting transfers between devices: 0.09 us -> 11.3 us
    reduce_scatter x2 -> x0, waiting for transfers between devices: 432 us -> none  [the longest x1 216 us: per_device(): lax.psum_scatter(jnp.dot(picked, w_down, preferred_element_type=jnp.float...]
    pallas_call x0 -> x1, Pallas kernels: none -> 109 us  [block(): pl.pallas_call(block_kernel, out_shape=jax.ShapeDtypeStruct((RB, D), BF16...]
    all_gather x1 -> x0, waiting for transfers between devices: 79.3 us -> none  [per_device(): piece_rows = lax.all_gather(normed, 'dp', axis=0, tiled=True)]
    all_to_all x1 -> x0, blocking collectives: 39.3 us -> none  [per_device(): lax.all_to_all(latent_out, 'dp', split_axis=1, concat_axis=0, tiled=True)]
    all_to_all x0 -> x1, waiting for transfers between devices: none -> 18.1 us  [per_device(): lax.all_to_all(latent_out, 'dp', split_axis=1, concat_axis=0, tiled=True)]
    dot_general x3 -> x0, matrix products: 14.7 us -> none  [the longest x1 7.84 us: per_device(): jnp.dot(picked, w_down, preferred_element_type=jnp.float32)]
    all_to_all x0 -> x1, starting transfers between devices: none -> 11.3 us  [per_device(): lax.all_to_all(latent_out, 'dp', split_axis=1, concat_axis=0, tiled=True)]
    unnamed x18 -> x13, local copies, waits for them, and re-layouts: 1.57 us -> 10.3 us
  transfers between devices with their start and end apart: 3 -> 1, of which waited for: 3 -> 1; matrix products, arithmetic and copies ran while one was open for 0% -> 6% of each run, Pallas kernels for 0% -> 0%
where the time goes in v1:
time: 162 us; the launch traced here: 161 us
  Pallas kernels  109 us (67%)
  waiting for transfers between devices  18.1 us (11%)
  local copies, waits for them, and re-layouts  13.7 us (8%)
  starting transfers between devices  11.3 us (7%)
  matrix products  6.86 us (4%)
  other arithmetic  1.97 us (1%)
    pallas_call x1, Pallas kernels, block(): pl.pallas_call(block_kernel, out_shape=jax.ShapeDtypeStruct((RB, D), BF16...  109 us
    all_to_all x1, waiting for transfers between devices, per_device(): lax.all_to_all(latent_out, 'dp', split_axis=1, concat_axis=0, tiled=True)  18.1 us
    all_to_all x1, starting transfers between devices, per_device(): lax.all_to_all(latent_out, 'dp', split_axis=1, concat_axis=0, tiled=True)  11.3 us
    unnamed x13, local copies, waits for them, and re-layouts  10.3 us
    dot_general x1, matrix products, per_device(): jnp.einsum('rhk,rck->rhc', query, cache, preferred_element_type=jnp.float32)  3.47 us
  transfers between devices with their start and end apart: 1, of which 1 were waited for; matrix products, arithmetic and copies ran while one was open for 6% of the time, Pallas kernels for 0%

profile of v1, /device:TPU:8, one launch (start us, length us, event | category | flops | bytes accessed | tf_op | source)
XLA Modules:
  0.0 161.4 jit_solution(1816153147229737734)
XLA Ops:
  0.0 0.0 copy-start
  0.0 0.8 iota_compare_fusion
  0.8 0.7 slice_convert_fusion
  1.6 0.0 copy-done
  1.6 0.0 slice-start
  1.6 1.4 fusion.10
  2.9 0.0 slice-start.1
  2.9 3.5 %fusion.13 = (f32[16,64]{1,0:T(8,128)S(1)}, f32[16,64,256]{2,1,0:T(8,128)S(1)}) fusion(bf16[16,64,576]{2,1,0:T(8,128)(2,1)S(1)} %copy-done, bf16[16,256,576]{1,2,0:T(8,128)(2,1)} %param.13, pred[16,256]{1,0:T(8,128)(4,1)S(1)} %iota_compare_fusion), kind=kOutput, calls=%fused_computation.19 | convolution fusion | flops 302775296 | bytes 6955008 | tf_op jit(solution)/shard_map/rhk,rck->rhc/dot_general | solution.py:409
  6.4 0.4 fusion.6
  6.9 0.0 slice-done
  6.9 0.0 slice-done.1
  6.9 1.6 divide_convert_fusion
  8.5 0.0 copy-start.2
  8.5 1.6 copy.19
  10.0 11.3 %all-to-all-start = ((bf16[16,64,512]{2,0,1:T(8,128)(2,1)}), bf16[16,64,512]{2,0,1:T(8,128)(2,1)S(1)}, u32[]{:S(2)}, u32[]{:S(2)}) async-start(bf16[16,64,512]{2,0,1:T(8,128)(2,1)} %copy.19), calls=%async_computation | async-start | bytes 2097152 | tf_op jit(solution)/shard_map/all_to_all | solution.py:431
  22.0 0.0 copy-done.2
  22.0 0.6 reshape.33.gain
  22.6 4.4 %copy.22.wg_hbm = bf16[3584,288]{1,0:T(8,128)(2,1)} copy(bf16[3584,288]{0,1:T(8,128)(2,1)} %param.21) | data formatting | bytes 4128768 | tf_op args[9]
  27.0 4.4 %copy.23.wu_hbm = bf16[3584,288]{1,0:T(8,128)(2,1)} copy(bf16[3584,288]{0,1:T(8,128)(2,1)} %param.22) | data formatting | bytes 4128768 | tf_op args[10]
  31.4 0.0 copy-start.1
  31.4 18.1 %all-to-all-done = bf16[16,64,512]{2,0,1:T(8,128)(2,1)S(1)} async-done(((bf16[16,64,512]{2,0,1:T(8,128)(2,1)}), bf16[16,64,512]{2,0,1:T(8,128)(2,1)S(1)}, u32[]{:S(2)}, u32[]{:S(2)}) %all-to-all-start) | async-done | bytes 1048608 | tf_op jit(solution)/shard_map/all_to_all | solution.py:431
  49.5 0.1 copy.20
  49.5 0.0 copy-done.1
  49.6 0.4 fusion.5
  50.0 0.3 copy.21
  50.3 0.9 reshape.32.heads
  51.2 108.7 %block.1 = bf16[16,3584]{1,0:T(8,128)(2,1)} custom-call(bf16[8,64,256]{2,1,0:T(8,128)(2,1)} %reshape.32.heads, bf16[16,3584]{1,0:T(8,128)(2,1)} %hidden.1, bf16[1,3584]{1,0:T(2,128)(2,1)} %reshape.33.gain, s32[1]{0:T(128)S(6)} %copy.30.counts, bf16[256,3584]{1,0:T(8,128)(2,1)} %wo_hbm.1, bf16[3584,288]{1,0:T(8,128)(2,1)} %copy.22.wg_hbm, ...), custom_call_target="tpu_custom_call" | custom-call | tf_op jit(solution)/shard_map/block/pallas_call | solution.py:368
  159.9 1.6 copy.31
  (3 shorter events, 0.0 us)
Async XLA Ops:
  0.0 1.6 copy-start
  1.6 5.3 %slice-start = ((s8[4718592]{0:T(1024)(128)(4,1)}), s8[4194304]{0:T(1024)(128)(4,1)S(1)}, s32[]{:S(2)}) async-start(s8[4718592]{0:T(1024)(128)(4,1)} %bitcast.14), calls=%async_computation.1 | async-start | bytes 8388608
  2.9 3.9 %slice-start.1 = ((s8[4718592]{0:T(1024)(128)(4,1)}), s8[524288]{0:T(1024)(128)(4,1)S(1)}, s32[]{:S(2)}) async-start(s8[4718592]{0:T(1024)(128)(4,1)} %bitcast.14), calls=%async_computation.2 | async-start | bytes 1048576
  8.5 13.6 %copy-start.2 = (bf16[3584]{0:T(1024)(128)(2,1)S(1)}, bf16[3584]{0:T(1024)(128)(2,1)}, u32[]{:S(2)}) copy-start(bf16[3584]{0:T(1024)(128)(2,1)} %param.20) | copy-start | bytes 21508
  10.0 39.4 %all-to-all-start = ((bf16[16,64,512]{2,0,1:T(8,128)(2,1)}), bf16[16,64,512]{2,0,1:T(8,128)(2,1)S(1)}, u32[]{:S(2)}, u32[]{:S(2)}) async-start(bf16[16,64,512]{2,0,1:T(8,128)(2,1)} %copy.19), calls=%async_computation | async-start | bytes 2097152 | tf_op jit(solution)/shard_map/all_to_all | solution.py:431
  31.4 18.2 %copy-start.1 = (bf16[2,512,128]{2,1,0:T(8,128)(2,1)S(1)}, bf16[2,512,128]{2,1,0:T(8,128)(2,1)}, u32[]{:S(2)}) copy-start(bf16[2,512,128]{2,1,0:T(8,128)(2,1)} %param.18) | copy-start | bytes 786436

commit v2 on v1

--- a/solution.py
+++ b/solution.py
@@ -13,6 +13,9 @@
 NZ, NX = 8, 4
 RB = 16
 D = 3584
+KVL = 512
+VHD = 128
+CTX = 256
 CA = 1792
 CB = D - CA
 HA, HB = CA // 2, CB // 2
@@ -127,7 +130,7 @@
     def first(i):
         k = RS_ORDER[i]
         c = net.zc(k)
-        make_part(c, part)
+        make_part(k, c, part)
         for h in range(2):
             cols = bcols(h)
             if k == 0:
@@ -288,8 +291,98 @@
         use_next()
 
 
-def block_kernel(
-    heads,
+class Inbox:
+    def __init__(self, send, sems, home):
+        self.send, self.sems, self.home = send, sems, home
+
+    def push(self, src, dst, index, dev):
+        self.send.start(src, dst, self.sems.at[(0, *index)], self.sems.at[(1, *index)], dev)
+
+    def wait(self, dst, index):
+        wait_recv(dst, self.sems.at[(0, *index)], self.sems.at[(1, *index)], self.home)
+
+
+class ValueUp:
+    def __init__(self, net, send, vu, z_sem, core_sem):
+        self.net, self.vu = net, vu
+        self.core = lax.rem(net.g, 2)
+        self.other = (net.g + 1 - 2 * self.core, net.z * NX + net.x)
+        home = net.zdev(0)
+        self.along = Inbox(send, z_sem, home)
+        self.across = Inbox(send, core_sem, home)
+
+    def ref(self, k, hops, d, head):
+        rows = slice(0, KVL) if hops < 4 else slice(d * (KVL // 2), (d + 1) * (KVL // 2))
+        return self.vu.at[self.net.zc(k), head, rows]
+
+    def start(self, hops):
+        for d, step in ((PLUS, 1), (MINUS, -1)):
+            ref = self.ref(-step * (hops - 1), hops, d, self.core)
+            self.along.push(ref, ref, (d, hops - 1), self.net.zdev(step))
+
+    def forward(self, hops):
+        for d, step in ((PLUS, 1), (MINUS, -1)):
+            ref = self.ref(-step * hops, hops, d, self.core)
+            self.along.wait(ref, (d, hops - 1))
+            self.across.push(ref, ref, (d, hops - 1), self.other)
+        if hops < 4:
+            self.start(hops + 1)
+
+    def finish(self):
+        for hops in range(1, 5):
+            for d, step in ((PLUS, 1), (MINUS, -1)):
+                self.across.wait(self.ref(-step * hops, hops, d, 1 - self.core), (d, hops - 1))
+
+
+def order_matrix(n, source):
+    i = lax.broadcasted_iota(jnp.int32, (n, n), 0)
+    j = lax.broadcasted_iota(jnp.int32, (n, n), 1)
+    return jnp.where(source(i) == j, 1.0, 0.0).astype(BF16)
+
+
+def attend(rs, query, cache, new_latent, lengths, order, lat):
+    qs = [query[r] for r in rs]
+    scores = [jnp.dot(q, cache[r], preferred_element_type=F32) * score_scale for q, r in zip(qs, rs)]
+    news = [new_latent[r : r + 1, :].astype(F32) for r in rs]
+    own = [
+        jnp.sum(q.astype(F32) * new, axis=-1, keepdims=True) * score_scale
+        for q, new in zip(qs, news)
+    ]
+    position = lax.broadcasted_iota(jnp.int32, (1, CTX), 1)
+    scores = [jnp.where(position < lengths[r], s, -jnp.inf) for s, r in zip(scores, rs)]
+    tops = [jnp.maximum(jnp.max(s, axis=-1, keepdims=True), o) for s, o in zip(scores, own)]
+    weights = [jnp.exp(s - top) for s, top in zip(scores, tops)]
+    own = [jnp.exp(o - top) for o, top in zip(own, tops)]
+    sums = [jnp.sum(w, axis=-1, keepdims=True) + o for w, o in zip(weights, own)]
+    mixed = [
+        lax.dot_general(
+            w.astype(BF16),
+            cache[r, 0:KVL, :],
+            (((1,), (1,)), ((), ())),
+            preferred_element_type=F32,
+        )
+        for w, r in zip(weights, rs)
+    ]
+    latent = [
+        ((m + o.astype(BF16).astype(F32) * new[:, 0:KVL]) * (1.0 / s)).astype(BF16)
+        for m, o, new, s in zip(mixed, own, news, sums)
+    ]
+    latent = [jnp.dot(order, value, preferred_element_type=F32).astype(BF16) for value in latent]
+    for value, r in zip(latent, rs):
+        for to in range(NX):
+            lat[to, r] = value[to * 16 : (to + 1) * 16]
+
+
+GROUPS = 4
+SIZE = RB // GROUPS
+
+
+def layer_kernel(
+    query_hbm,
+    cache_hbm,
+    new_latent,
+    lengths,
+    vu_hbm,
     hidden,
     gain,
     counts,
@@ -298,6 +391,21 @@
     wu_hbm,
     wd_hbm,
     out,
+    query,
+    cache,
+    vu,
+    lat,
+    lat_in,
+    by_head,
+    heads_out,
+    heads,
+    q_sem,
+    c_sem,
+    v_sem,
+    lat_sem,
+    heads_sem,
+    vz_sem,
+    vcore_sem,
     wo,
     wg,
     wu,
@@ -310,22 +418,84 @@
 ):
     rs1, rs2, ag = scratch[:N_RS], scratch[N_RS : 2 * N_RS], scratch[2 * N_RS :]
     net = Net()
+    z, x = net.z, net.x
+    home = net.zdev(0)
     send = Sender()
+
+    loads = []
+    for i in range(GROUPS):
+        part = pl.ds(i * SIZE, SIZE)
+        loads.append(
+            (
+                pltpu.make_async_copy(query_hbm.at[part], query.at[part], q_sem.at[i]),
+                pltpu.make_async_copy(cache_hbm.at[part], cache.at[part], c_sem.at[i]),
+            )
+        )
+    own_vu = pltpu.make_async_copy(vu_hbm, vu.at[z], v_sem.at[0])
     weights = [
         pltpu.make_async_copy(src, dst, w_sem.at[i])
         for i, (src, dst) in enumerate(((wo_hbm, wo), (wg_hbm, wg), (wu_hbm, wu), (wd_hbm, wd)))
     ]
-    for copy in weights:
+    for copy in [own_vu, *loads[0], *loads[1], *loads[2], *loads[3], *weights]:
         copy.start()
+
+    value_up = ValueUp(net, send, vu, vz_sem, vcore_sem)
+    z_others = (4, -3, 3, -2, 2, -1, 1)
     barrier = pltpu.get_barrier_semaphore()
-    partners = [net.zdev(1), net.zdev(-1)] + [net.xdev(o) for o in (1, 2, 3)]
+    partners = [net.zdev(k) for k in z_others] + [net.xdev(o) for o in (1, 2, 3)] + [value_up.other]
     for dev in partners:
         pl.semaphore_signal(barrier, inc=1, device_id=dev, device_id_type=MESH)
     pl.semaphore_wait(barrier, len(partners))
 
+    own_vu.wait()
+    value_up.start(1)
+
+    order = order_matrix(
+        64, lambda i: ((i & 15) >> 1) * 8 + (i >> 4) * 2 + (i & 1)
+    )
+    lat_box = Inbox(send, lat_sem, home)
+    for i in range(GROUPS):
+        for copy in loads[i]:
+            copy.wait()
+        attend(range(i * SIZE, (i + 1) * SIZE), query, cache, new_latent, lengths, order, lat)
+        part = pl.ds(i * SIZE, SIZE)
+        for o in (1, 3, 2):
+            lat_box.push(lat.at[net.xc(o), part], lat_in.at[o - 1, part], (o - 1, i), net.xdev(o))
+        if i % 2:
+            value_up.forward(i // 2 + 1)
+
+    swap = order_matrix(256, lambda i: ((i & 15) << 4) + (i >> 4))
+
+    def sort(o):
+        rows = lat[x] if o == 0 else lat_in[o - 1]
+        value = jnp.dot(swap, rows.reshape(RB * 16, KVL), preferred_element_type=F32)
+        by_head[:, net.xc(-o)] = value.astype(BF16).reshape(16, RB, KVL)
+
+    sort(0)
+    value_up.forward(3)
+    for o in (1, 3, 2):
+        for i in range(GROUPS):
+            lat_box.wait(lat_in.at[o - 1, pl.ds(i * SIZE, SIZE)], (o - 1, i))
+        sort(o)
+    value_up.forward(4)
+    value_up.finish()
+
+    heads_box = Inbox(send, heads_sem, home)
+    for i, k in enumerate((*z_others, 0)):
+        c = net.zc(k)
+        target = heads if k == 0 else heads_out
+        for j in range(2):
+            rows = by_head[c * 2 + j].reshape(NX * RB, KVL)
+            value = jnp.dot(rows, vu[c, j], preferred_element_type=F32)
+            target[c, :, j * VHD : (j + 1) * VHD] = value.astype(BF16)
+        if k:
+            heads_box.push(heads_out.at[c], heads.at[z], (i,), net.zdev(k))
+
     weights[0].wait()
 
-    def project(c, part):
+    def project(k, c, part):
+        if k:
+            heads_box.wait(heads.at[c], (z_others.index(-k if k < 4 else 4),))
         value = jnp.dot(heads[c], wo[...], preferred_element_type=F32)
         part[c] = value.astype(BF16).reshape(NX, RB, D)
 
@@ -335,22 +505,23 @@
     rows = ag[0]
     residual = total[...]
     mean_sq = jnp.mean(residual * residual, axis=-1, keepdims=True)
-    rows[net.z, net.x] = (residual * lax.rsqrt(mean_sq + 1e-06) * gain[...].astype(F32)).astype(BF16)
+    rows[z, x] = (residual * lax.rsqrt(mean_sq + 1e-06) * gain[...].astype(F32)).astype(BF16)
 
     weights[1].wait()
     weights[2].wait()
 
     def feed(c):
         chunk = rows[c].reshape(NX * RB, D)
-        gate = jnp.dot(chunk, wg[...], preferred_element_type=F32)
-        up = jnp.dot(chunk, wu[...], preferred_element_type=F32)
+        dims = (((1,), (1,)), ((), ()))
+        gate = lax.dot_general(chunk, wg[...], dims, preferred_element_type=F32)
+        up = lax.dot_general(chunk, wu[...], dims, preferred_element_type=F32)
         inner[c] = (gate / (1.0 + jnp.exp(-gate)) * up).astype(BF16)
 
     all_gather(net, send, feed, ag)
 
     weights[3].wait()
 
-    def down(c, part):
+    def down(k, c, part):
         value = jnp.dot(inner[c], wd[...], preferred_element_type=F32)
         part[c] = value.astype(BF16).reshape(NX, RB, D)
 
@@ -359,35 +530,6 @@
     live = lax.broadcasted_iota(jnp.int32, (RB, D), 0) < counts[0]
     out[...] = jnp.where(live, ffn[...], 0.0).astype(BF16)
     send.finish()
-
-
-def block(heads, hidden, gain, counts, wo, wg, wu, wd):
-    vmem = pl.BlockSpec(memory_space=pltpu.VMEM)
-    hbm = pl.BlockSpec(memory_space=pl.ANY)
-    n_inner = wg.shape[1]
-    return pl.pallas_call(
-        block_kernel,
-        out_shape=jax.ShapeDtypeStruct((RB, D), BF16),
-        in_specs=[vmem, vmem, vmem, pl.BlockSpec(memory_space=pltpu.SMEM), hbm, hbm, hbm, hbm],
-        out_specs=vmem,
-        scratch_shapes=[
-            pltpu.VMEM(wo.shape, BF16),
-            pltpu.VMEM(wg.shape, BF16),
-            pltpu.VMEM(wu.shape, BF16),
-            pltpu.VMEM(wd.shape, BF16),
-            pltpu.SemaphoreType.DMA((4,)),
-            pltpu.VMEM((NZ, NX * RB, n_inner), BF16),
-            pltpu.VMEM((RB, D), F32),
-            pltpu.VMEM((RB, D), F32),
-            *RS_SCRATCH,
-            *RS_SCRATCH,
-            *AG_SCRATCH,
-        ],
-        compiler_params=pltpu.CompilerParams(
-            collective_id=1, has_side_effects=True, vmem_limit_bytes=56 << 20
-        ),
-        name="block",
-    )(heads, hidden, gain, counts, wo, wg, wu, wd)
 
 
 def per_device(
@@ -404,37 +546,61 @@
     w_up,
     w_down,
 ):
-    latent_width = value_up.shape[1]
-    scores = (
-        jnp.einsum("rhk,rck->rhc", query, cache, preferred_element_type=jnp.float32) * score_scale
-    )
-    self_score = (
-        jnp.einsum("rhk,rk->rh", query, new_latent, preferred_element_type=jnp.float32)
-        * score_scale
-    )
-    positions = jnp.arange(cache.shape[1], dtype=jnp.int32)
-    in_range = positions[None, None, :] < lengths[:, None, None]
-    scores = jnp.where(in_range, scores, -jnp.inf)
-    row_max = jnp.maximum(jnp.max(scores, axis=-1), self_score)
-    weights = jnp.exp(scores - row_max[..., None])
-    self_weight = jnp.exp(self_score - row_max)
-    denom_sum = jnp.sum(weights, axis=-1) + self_weight
-    weights_b = weights.astype(jnp.bfloat16)
-    self_b = self_weight.astype(jnp.bfloat16).astype(jnp.float32)
-    mixed_sum = jnp.einsum(
-        "rhc,rcl->rhl", weights_b, cache[:, :, :latent_width], preferred_element_type=jnp.float32
-    )
-    mixed_sum = mixed_sum + self_b[..., None] * new_latent[:, None, :latent_width].astype(
-        jnp.float32
-    )
-    latent_out = (mixed_sum / denom_sum[..., None]).astype(jnp.bfloat16)
-    exchanged = lax.all_to_all(latent_out, "dp", split_axis=1, concat_axis=0, tiled=True)
-    heads_out = jnp.einsum(
-        "rhl,hlv->rhv", exchanged, value_up, preferred_element_type=jnp.float32
-    ).astype(jnp.bfloat16)
-    heads = heads_out.reshape(NZ, NX * RB, -1)
-    return block(
-        heads, hidden_in, norm_gain.reshape(1, D), counts, out_proj, w_gate, w_up, w_down
+    cache = cache.transpose(0, 2, 1)
+    w_gate, w_up = w_gate.T, w_up.T
+    vmem = pl.BlockSpec(memory_space=pltpu.VMEM)
+    smem = pl.BlockSpec(memory_space=pltpu.SMEM)
+    hbm = pl.BlockSpec(memory_space=pl.ANY)
+    return pl.pallas_call(
+        layer_kernel,
+        out_shape=jax.ShapeDtypeStruct((RB, D), BF16),
+        in_specs=[hbm, hbm, vmem, smem, hbm, vmem, vmem, smem, hbm, hbm, hbm, hbm],
+        out_specs=vmem,
+        scratch_shapes=[
+            pltpu.VMEM(query.shape, BF16),
+            pltpu.VMEM(cache.shape, BF16),
+            pltpu.VMEM((NZ, 2, KVL, VHD), BF16),
+            pltpu.VMEM((NX, RB, 16, KVL), BF16),
+            pltpu.VMEM((3, RB, 16, KVL), BF16),
+            pltpu.VMEM((16, NX, RB, KVL), BF16),
+            pltpu.VMEM((NZ, NX * RB, 2 * VHD), BF16),
+            pltpu.VMEM((NZ, NX * RB, 2 * VHD), BF16),
+            pltpu.SemaphoreType.DMA((GROUPS,)),
+            pltpu.SemaphoreType.DMA((GROUPS,)),
+            pltpu.SemaphoreType.DMA((1,)),
+            pltpu.SemaphoreType.DMA((2, 3, GROUPS)),
+            pltpu.SemaphoreType.DMA((2, 7)),
+            pltpu.SemaphoreType.DMA((2, 2, 4)),
+            pltpu.SemaphoreType.DMA((2, 2, 4)),
+            pltpu.VMEM(out_proj.shape, BF16),
+            pltpu.VMEM(w_gate.shape, BF16),
+            pltpu.VMEM(w_up.shape, BF16),
+            pltpu.VMEM(w_down.shape, BF16),
+            pltpu.SemaphoreType.DMA((4,)),
+            pltpu.VMEM((NZ, NX * RB, w_gate.shape[0]), BF16),
+            pltpu.VMEM((RB, D), F32),
+            pltpu.VMEM((RB, D), F32),
+            *RS_SCRATCH,
+            *RS_SCRATCH,
+            *AG_SCRATCH,
+        ],
+        compiler_params=pltpu.CompilerParams(
+            collective_id=1, has_side_effects=True, vmem_limit_bytes=60 << 20
+        ),
+        name="layer",
+    )(
+        query,
+        cache,
+        new_latent,
+        lengths,
+        value_up,
+        hidden_in,
+        norm_gain.reshape(1, D),
+        counts,
+        out_proj,
+        w_gate,
+        w_up,
+        w_down,
     )
 
 

time: 162 us -> 149 us (0.920)
  Pallas kernels: 109 us -> 145 us
  waiting for transfers between devices: 18.1 us -> 0 us
  starting transfers between devices: 11.3 us -> 0 us
  local copies, waits for them, and re-layouts: 13.7 us -> 2.86 us
  matrix products: 6.86 us -> 0 us
  other arithmetic: 1.97 us -> 0 us
    pallas_call x1, Pallas kernels: 109 us -> 145 us  [per_device(): pl.pallas_call(layer_kernel, out_shape=jax.ShapeDtypeStruct((RB, D), BF16...]
    all_to_all x1 -> x0, waiting for transfers between devices: 18.1 us -> none  [per_device(): lax.all_to_all(latent_out, 'dp', split_axis=1, concat_axis=0, tiled=True)]
    all_to_all x1 -> x0, starting transfers between devices: 11.3 us -> none  [per_device(): lax.all_to_all(latent_out, 'dp', split_axis=1, concat_axis=0, tiled=True)]
    unnamed x13 -> x1, local copies, waits for them, and re-layouts: 10.3 us -> 1.55 us
    dot_general x4 -> x0, matrix products: 6.86 us -> none  [the longest x1 3.47 us: per_device(): jnp.einsum('rhk,rck->rhc', query, cache, preferred_element_type=jnp.float32)]
    convert_element_type x2 -> x0, local copies, waits for them, and re-layouts: 1.84 us -> none  [the longest x1 1.57 us: per_device(): latent_out = (mixed_sum / denom_sum[..., None]).astype(jnp.bfloat16)]
  transfers between devices with their start and end apart: 1 -> 0, of which waited for: 1 -> 0; matrix products, arithmetic and copies ran while one was open for 6% -> 0% of each run, Pallas kernels for 0% -> 0%
where the time goes in v2:
time: 149 us
  Pallas kernels  145 us (97%)
  local copies, waits for them, and re-layouts  2.86 us (2%)
    pallas_call x1, Pallas kernels, per_device(): pl.pallas_call(layer_kernel, out_shape=jax.ShapeDtypeStruct((RB, D), BF16...  145 us

profile of v2, /device:TPU:8, one launch (start us, length us, event | category | flops | bytes accessed | tf_op | source)
XLA Modules:
  0.0 148.5 jit_solution(11335370272527938914)
XLA Ops:
  0.7 1.3 reshape.3.gain
  2.0 145.0 %layer.1 = bf16[16,3584]{1,0:T(8,128)(2,1)} custom-call(bf16[16,64,576]{2,1,0:T(8,128)(2,1)} %query_hbm.1, bf16[16,576,256]{2,1,0:T(8,128)(2,1)} %bitcast.3, bf16[16,576]{1,0:T(8,128)(2,1)} %new_latent.1, s32[16]{0:T(128)} %lengths.1, bf16[2,512,128]{2,1,0:T(8,128)(2,1)} %vu_hbm.1, bf16[16,3584]{1,0:T(8,128)(2,1)} %hidden.1, bf16[1,3584]{1,0:T(2,128)(2,1)} %reshape.3.gain, ...), custom_call_target="tpu_custom_call" | custom-call | tf_op jit(solution)/shard_map/layer/pallas_call | solution.py:554
  147.0 1.6 %copy.15 = bf16[16,3584]{1,0:T(8,128)(2,1)} copy(bf16[16,3584]{1,0:T(8,128)(2,1)} %layer.1) | data formatting | bytes 229376

commit v3 on v2

v3 whole, which is shorter than its diff:
```python
import jax
import jax.numpy as jnp
from jax import lax
from jax.experimental import pallas as pl
from jax.experimental.pallas import tpu as pltpu
from jax.sharding import PartitionSpec as P

score_scale = 192.0 ** (-0.5)
MESH = pl.DeviceIdType.MESH
F32 = jnp.float32
BF16 = jnp.bfloat16

NZ, NX, NY = 8, 4, 4
RB = 16
ZB = NX * RB
D = 3584
DX = D // NX
KVL = 512
VHD = 128
CTX = 256
FD = 288
FM, FR, FREP = 256, 32, 4
FK = FM + FR * FREP
CA = 384
PLUS, MINUS = 0, 1
TREE_A, TREE_H, TREE_I = False, False, False
EARLY = False
FAR = True
STEP = (1, -1)
XO = (1, 3, 2)
RS_ORDER = (4, -3, 3, -2, 2, -1, 1, 0)


def half(h):
    return slice(h * ZB // 2, (h + 1) * ZB // 2)


class Net:
    def __init__(self):
        self.g = lax.axis_index("grp")
        self.d = lax.axis_index("dp")
        self.z = self.d // NX
        self.x = lax.rem(self.d, NX)
        self.y = self.g // 2
        self.core = lax.rem(self.g, 2)
        self.sibling = (self.g + 1 - 2 * self.core, self.d)

    def zc(self, k):
        return lax.rem(self.z + (k + NZ), NZ)

    def xc(self, k):
        return lax.rem(self.x + (k + NX), NX)

    def yc(self, k):
        return lax.rem(self.y + (k + NY), NY)

    def zdev(self, k):
        return (self.g, self.zc(k) * NX + self.x)

    def xdev(self, k):
        return (self.g, self.z * NX + self.xc(k))

    def ydev(self, k):
        return (self.yc(k) * 2 + self.core, self.d)


def xcols(q):
    if isinstance(q, int):
        return slice(q * DX, (q + 1) * DX)
    return pl.ds(pl.multiple_of(q * DX, 128), DX)


class Sender:
    def __init__(self):
        self.started = []

    def start(self, src, dst, ssem, rsem, dev):
        copy = pltpu.make_async_remote_copy(
            src_ref=src,
            dst_ref=dst,
            send_sem=ssem,
            recv_sem=rsem,
            device_id=dev,
            device_id_type=MESH,
        )
        copy.start()
        self.started.append(copy)

    def finish(self):
        for copy in self.started:
            copy.wait_send()


def wait_recv(dst, ssem, rsem, dev):
    pltpu.make_async_remote_copy(
        src_ref=dst,
        dst_ref=dst,
        send_sem=ssem,
        recv_sem=rsem,
        device_id=dev,
        device_id_type=MESH,
    ).wait_recv()


class Inbox:
    def __init__(self, send, sems, home):
        self.send, self.sems, self.home = send, sems, home

    def push(self, src, dst, index, dev):
        self.send.start(src, dst, self.sems.at[(0, *index)], self.sems.at[(1, *index)], dev)

    def wait(self, dst, index):
        wait_recv(dst, self.sems.at[(0, *index)], self.sems.at[(1, *index)], self.home)


class AlongX:
    def __init__(self, net, send, block, sem, tree):
        self.net, self.block = net, block
        self.box = Inbox(send, sem, net.zdev(0))
        self.tree = tree

    def relayed(self, k):
        return self.tree and k != 4

    def push(self, k):
        i = RS_ORDER.index(k)
        ref = self.block(k, self.net.x, None)
        for d in (PLUS, MINUS):
            self.box.push(ref, ref, (i, d, 0), self.net.xdev(STEP[d]))
        if not self.relayed(k):
            self.box.push(ref, ref, (i, 0, 1), self.net.xdev(2))

    def relay(self, k, last=False):
        if not (self.relayed(k) or last):
            return
        i = RS_ORDER.index(k)
        for d in (PLUS, MINUS):
            come = self.net.xc(-STEP[d])
            self.box.wait(self.block(k, come, None), (i, d, 0))
            if not last:
                ref = self.block(k, come, d)
                self.box.push(ref, ref, (i, d, 1), self.net.xdev(STEP[d]))

    def finish(self, k):
        i = RS_ORDER.index(k)
        if not self.relayed(k):
            self.relay(k, True)
            self.box.wait(self.block(k, self.net.xc(2), None), (i, 0, 1))
            return
        for d in (PLUS, MINUS):
            self.box.wait(self.block(k, self.net.xc(2), d), (i, d, 1))


ALONG_X_SEM = pltpu.SemaphoreType.DMA((2, NZ, 2, 2))


class Regroup:
    def __init__(self, net, send, own, buf, x_sem, y_sem, core_sem):
        self.net, self.own, self.buf = net, own, buf
        home = net.zdev(0)
        self.over_x = Inbox(send, x_sem, home)
        self.over_y = Inbox(send, y_sem, home)
        self.across = Inbox(send, core_sem, home)

    def start(self):
        net = self.net
        for o in XO:
            src = self.own.at[:, xcols(net.xc(o))]
            self.over_x.push(src, self.buf.at[net.x, net.g], (o - 1,), net.xdev(o))
        self.buf[net.x, net.g] = self.own[:, xcols(net.x)]

    def spread(self):
        net = self.net
        for o in XO:
            self.over_x.wait(self.buf.at[net.xc(-o), net.g], (o - 1,))
        ref = self.buf.at[:, net.g]
        for o in XO:
            self.over_y.push(ref, ref, (o - 1,), net.ydev(o))
        self.across.push(ref, ref, (0,), net.sibling)

    def pass_on(self):
        net = self.net
        for o in XO:
            ref = self.buf.at[:, net.yc(-o) * 2 + net.core]
            self.over_y.wait(ref, (o - 1,))
            self.across.push(ref, ref, (o,), net.sibling)

    def finish(self):
        net = self.net
        for o in range(NY):
            self.across.wait(self.buf.at[:, net.yc(-o) * 2 + 1 - net.core], (o,))


REGROUP_SEMS = [
    pltpu.SemaphoreType.DMA((2, 3)),
    pltpu.SemaphoreType.DMA((2, 3)),
    pltpu.SemaphoreType.DMA((2, 4)),
]

SUM_SCRATCH = [
    pltpu.VMEM((NZ, ZB, DX), BF16),
    pltpu.VMEM((2, 4, 2, ZB // 2, DX), BF16),
    pltpu.SemaphoreType.DMA((2, 2, 4, 2)),
]


class SumZ:
    def __init__(self, net, send, part, came, sem):
        self.net, self.part, self.came = net, part, came
        self.box = Inbox(send, sem, net.zdev(0))

    def step(self, k, term, chained=True):
        c = self.net.zc(k)
        d = PLUS if k > 0 else MINUS
        for h in (0, 1) if k == 4 else (1 - d, d):
            value = term[half(h)]
            hops = abs(k)
            if k == 4:
                d = h
            elif hops < 3 or (chained and h == d):
                self.box.wait(self.came.at[d, hops, h], (d, hops, h))
                value = value + self.came[d, hops, h].astype(F32)
            self.part[c, half(h)] = value.astype(BF16)
            self.box.push(
                self.part.at[c, half(h)],
                self.came.at[d, hops - 1, h],
                (d, hops - 1, h),
                self.net.zdev(STEP[d]),
            )

    def last(self, h):
        for d in (PLUS, MINUS):
            self.box.wait(self.came.at[d, 0, h], (d, 0, h))
        return self.came[PLUS, 0, h].astype(F32) + self.came[MINUS, 0, h].astype(F32)


AG_SCRATCH = [
    pltpu.VMEM((NZ, NX, ZB, DX), BF16),
    ALONG_X_SEM,
    pltpu.SemaphoreType.DMA((2, 2, 4)),
    pltpu.SemaphoreType.DMA((2, 2, 4, 2)),
    pltpu.SemaphoreType.DMA((2, 3)),
]


def all_gather(net, send, use, between, rows, ax_sem, az_sem, bz_sem, bx_sem):
    z, x = net.z, net.x
    home = net.zdev(0)
    az, bz, bx = (Inbox(send, sem, home) for sem in (az_sem, bz_sem, bx_sem))

    def a_block(k, q, h):
        return rows.at[net.zc(k), q, slice(0, ZB) if h is None else half(h), 0:CA]

    ax = AlongX(net, send, a_block, ax_sem, TREE_A)

    def a_ref(k, hops, d):
        return rows.at[net.zc(k), x, slice(0, ZB) if hops < 4 else half(d), 0:CA]

    def a_send(hops, d):
        ref = a_ref(-STEP[d] * (hops - 1), hops, d)
        az.push(ref, ref, (d, hops - 1), net.zdev(STEP[d]))

    def b_ref(k, h):
        return rows.at[net.zc(k), :, half(h), CA:DX]

    def b_send(hops, d, h):
        ref = b_ref(-STEP[d] * (hops - 1), h)
        bz.push(ref, ref, (d, hops - 1, h), net.zdev(STEP[d]))

    def step_a(hops):
        for d in (PLUS, MINUS):
            az.wait(a_ref(-STEP[d] * hops, hops, d), (d, hops - 1))
            if hops < 4:
                a_send(hops + 1, d)
                ax.push(-STEP[d] * hops)
        if hops == 4:
            ax.push(4)

    def step_b(hops, far):
        for d in (PLUS, MINUS):
            h = d if far else 1 - d
            bz.wait(b_ref(-STEP[d] * hops, h), (d, hops - 1, h))
            if hops < 3 or (hops == 3 and far):
                b_send(hops + 1, d, h)

    def finish(k):
        ax.finish(k)
        use(k)

    for d in (PLUS, MINUS):
        a_send(1, d)
    own_b = rows.at[z, x, :, CA:DX]
    for o in XO:
        bx.push(own_b, own_b, (o - 1,), net.xdev(o))
    ax.push(0)
    step_a(1)
    for o in XO:
        bx.wait(rows.at[z, net.xc(-o), :, CA:DX], (o - 1,))
    for far in (True, False):
        for d in (PLUS, MINUS):
            b_send(1, d, d if far else 1 - d)
    ax.relay(0)
    step_a(2)
    ax.relay(-1)
    ax.relay(1)
    finish(0)
    step_b(1, True)
    step_a(3)
    ax.relay(-2)
    ax.relay(2)
    step_b(1, False)
    step_a(4)
    finish(-1)
    ax.relay(-3)
    ax.relay(3)
    finish(1)
    step_b(2, True)
    ax.relay(4)
    step_b(2, False)
    finish(-2)
    step_b(3, True)
    finish(2)
    step_b(3, False)
    between(0)
    finish(-3)
    finish(3)
    step_b(4, True)
    between(1)
    finish(4)


class ValueUp:
    def __init__(self, net, send, vu, z_sem, core_sem):
        self.net, self.vu = net, vu
        self.core, self.other = net.core, net.sibling
        home = net.zdev(0)
        self.along = Inbox(send, z_sem, home)
        self.across = Inbox(send, core_sem, home)

    def ref(self, k, hops, d, head):
        rows = slice(0, KVL) if hops < 4 else slice(d * (KVL // 2), (d + 1) * (KVL // 2))
        return self.vu.at[self.net.zc(k), head, rows]

    def start(self, hops):
        for d, step in ((PLUS, 1), (MINUS, -1)):
            ref = self.ref(-step * (hops - 1), hops, d, self.core)
            self.along.push(ref, ref, (d, hops - 1), self.net.zdev(step))

    def forward(self, hops):
        for d, step in ((PLUS, 1), (MINUS, -1)):
            ref = self.ref(-step * hops, hops, d, self.core)
            self.along.wait(ref, (d, hops - 1))
            self.across.push(ref, ref, (d, hops - 1), self.other)
        if hops < 4:
            self.start(hops + 1)

    def finish(self):
        for hops in range(1, 5):
            for d, step in ((PLUS, 1), (MINUS, -1)):
                self.across.wait(self.ref(-step * hops, hops, d, 1 - self.core), (d, hops - 1))


def order_matrix(n, source):
    i = lax.broadcasted_iota(jnp.int32, (n, n), 0)
    j = lax.broadcasted_iota(jnp.int32, (n, n), 1)
    return jnp.where(source(i) == j, 1.0, 0.0).astype(BF16)


def attend(rs, query, cache, new_latent, lengths, order, lat):
    qs = [query[r] for r in rs]
    scores = [jnp.dot(q, cache[r], preferred_element_type=F32) * score_scale for q, r in zip(qs, rs)]
    news = [new_latent[r : r + 1, :].astype(F32) for r in rs]
    own = [
        jnp.sum(q.astype(F32) * new, axis=-1, keepdims=True) * score_scale
        for q, new in zip(qs, news)
    ]
    position = lax.broadcasted_iota(jnp.int32, (1, CTX), 1)
    scores = [jnp.where(position < lengths[r], s, -jnp.inf) for s, r in zip(scores, rs)]
    tops = [jnp.maximum(jnp.max(s, axis=-1, keepdims=True), o) for s, o in zip(scores, own)]
    weights = [jnp.exp(s - top) for s, top in zip(scores, tops)]
    own = [jnp.exp(o - top) for o, top in zip(own, tops)]
    sums = [jnp.sum(w, axis=-1, keepdims=True) + o for w, o in zip(weights, own)]
    mixed = [
        lax.dot_general(
            w.astype(BF16),
            cache[r, 0:KVL, :],
            (((1,), (1,)), ((), ())),
            preferred_element_type=F32,
        )
        for w, r in zip(weights, rs)
    ]
    latent = [
        ((m + o.astype(BF16).astype(F32) * new[:, 0:KVL]) * (1.0 / s)).astype(BF16)
        for m, o, new, s in zip(mixed, own, news, sums)
    ]
    latent = [jnp.dot(order, value, preferred_element_type=F32).astype(BF16) for value in latent]
    for value, r in zip(latent, rs):
        for to in range(NX):
            lat[to, r] = value[to * 16 : (to + 1) * 16]


GROUPS = 4
SIZE = RB // GROUPS


def layer_kernel(
    query_hbm,
    cache_hbm,
    new_latent,
    lengths,
    vu_hbm,
    hidden,
    gain,
    counts,
    wo_hbm,
    wg_hbm,
    wu_hbm,
    wd_hbm,
    out,
    query,
    cache,
    vu,
    lat,
    lat_in,
    by_head,
    heads_out,
    heads,
    q_sem,
    c_sem,
    lat_sem,
    heads_sem,
    heads_x_sem,
    vz_sem,
    vcore_sem,
    wo_own,
    wo,
    wd_own,
    wd_in,
    wd,
    wg,
    wu,
    own_sem,
    w_sem,
    inner,
    inner_sem,
    hid,
    hid_sem,
    square,
    square_in,
    square_sem,
    total,
    result,
    result_in,
    result_sem,
    far,
    far_in,
    far_sem,
    *scratch,
):
    net = Net()
    z, x = net.z, net.x
    home = net.zdev(0)
    send = Sender()
    sum_heads = SumZ(net, send, *scratch[0:3])
    sum_ffn = SumZ(net, send, *scratch[3:6])
    wo_group = Regroup(net, send, wo_own, wo, *scratch[6:9])
    wd_group = Regroup(net, send, wd_own, wd_in, *scratch[9:12])
    ag = scratch[12:]

    z_others = RS_ORDER[:-1]
    barrier = pltpu.get_barrier_semaphore()
    partners = [net.zdev(k) for k in z_others] + [net.xdev(o) for o in XO]
    partners += [net.ydev(o) for o in XO] + [net.sibling]
    for dev in partners:
        pl.semaphore_signal(barrier, inc=1, device_id=dev, device_id_type=MESH)

    loads = []
    for i in range(GROUPS):
        part = pl.ds(i * SIZE, SIZE)
        loads.append(
            (
                pltpu.make_async_copy(query_hbm.at[part], query.at[part], q_sem.at[i]),
                pltpu.make_async_copy(cache_hbm.at[part], cache.at[part], c_sem.at[i]),
            )
        )
    own_vu = pltpu.make_async_copy(vu_hbm, vu.at[z], own_sem.at[0])
    own_wo = pltpu.make_async_copy(
        wo_hbm.at[pl.ds(pl.multiple_of(net.g * 32, 32), 32)], wo_own, own_sem.at[1]
    )
    own_wd = pltpu.make_async_copy(
        wd_hbm.at[pl.ds(pl.multiple_of(net.y * 64 + net.core * 48, 16), 48)], wd_own, own_sem.at[2]
    )
    weights = []
    for i, (src, dst) in enumerate(((wg_hbm, wg), (wu_hbm, wu))):
        weights.append(pltpu.make_async_copy(src, dst.at[0:FD], w_sem.at[i, 0]))
        for j in range(1, FREP):
            weights.append(
                pltpu.make_async_copy(
                    src.at[FM:FD], dst.at[FM + j * FR : FM + (j + 1) * FR], w_sem.at[i, j]
                )
            )

    def begin(copies):
        for copy in copies:
            copy.start()

    begin([*loads[0], own_vu, own_wo, *loads[1]])

    value_up = ValueUp(net, send, vu, vz_sem, vcore_sem)
    order = order_matrix(
        64, lambda i: ((i & 15) >> 1) * 8 + (i >> 4) * 2 + (i & 1)
    )
    lat_box = Inbox(send, lat_sem, home)
    hid_box = Inbox(send, hid_sem, home)
    later = ([*loads[2]], [*loads[3]], [own_wd], weights)
    for i in range(GROUPS):
        for copy in loads[i]:
            copy.wait()
        begin(later[i])
        attend(range(i * SIZE, (i + 1) * SIZE), query, cache, new_latent, lengths, order, lat)
        if i == 0:
            own_vu.wait()
            own_wo.wait()
            pl.semaphore_wait(barrier, len(partners))
            value_up.start(1)
            wo_group.start()
        part = pl.ds(i * SIZE, SIZE)
        for o in XO:
            lat_box.push(lat.at[net.xc(o), part], lat_in.at[o - 1, part], (o - 1, i), net.xdev(o))
        if i == 1:
            wo_group.spread()
            value_up.forward(1)
    for o in XO:
        hid_box.push(hidden.at[:, xcols(net.xc(o))], hid.at[x], (o - 1,), net.xdev(o))
    hid[x] = hidden[:, xcols(x)]
    value_up.forward(2)

    swap = order_matrix(256, lambda i: ((i & 15) << 4) + (i >> 4))

    def sort(o):
        rows = lat[x] if o == 0 else lat_in[o - 1]
        value = jnp.dot(swap, rows.reshape(RB * 16, KVL), preferred_element_type=F32)
        by_head[:, net.xc(-o)] = value.astype(BF16).reshape(16, RB, KVL)

    sort(0)
    value_up.forward(3)
    wo_group.pass_on()
    for o in XO:
        for i in range(GROUPS):
            lat_box.wait(lat_in.at[o - 1, pl.ds(i * SIZE, SIZE)], (o - 1, i))
        sort(o)
    own_wd.wait()
    wd_group.start()
    value_up.forward(4)
    value_up.finish()

    heads_box = Inbox(send, heads_sem, home)
    for i, k in enumerate(RS_ORDER):
        c = net.zc(k)
        for j in range(2):
            rows = by_head[c * 2 + j].reshape(ZB, KVL)
            value = jnp.dot(rows, vu[c, j], preferred_element_type=F32).astype(BF16)
            cols = slice(j * VHD, (j + 1) * VHD)
            if k:
                heads_out[c, :, cols] = value
            else:
                heads[z, x, :, cols] = value
        if k:
            heads_box.push(heads_out.at[c], heads.at[z, x], (i,), net.zdev(k))

    def heads_block(k, q, h):
        return heads.at[net.zc(k), q, slice(0, ZB) if h is None else half(h)]

    heads_x = AlongX(net, send, heads_block, heads_x_sem, TREE_H)

    def project(k):
        c = net.zc(k)
        heads_x.finish(k)
        rows = jnp.concatenate([heads[c, q] for q in range(NX)], axis=1)
        term = jnp.dot(rows, wo[...].reshape(NX * 256, DX), preferred_element_type=F32)
        if k:
            sum_heads.step(k, term)
            return
        for o in XO:
            hid_box.wait(hid.at[net.xc(-o)], (o - 1,))
        for h in range(2):
            before = hid[2 * h : 2 * h + 2].reshape(ZB // 2, DX).astype(F32)
            total[half(h)] = before + (term[half(h)] + sum_heads.last(h))

    for i, k in enumerate(RS_ORDER):
        if k:
            heads_box.wait(heads.at[net.zc(k), x], (z_others.index(-k if k < 4 else 4),))
        heads_x.push(k)
        if i == 2 and EARLY:
            wo_group.finish()
        if i:
            heads_x.relay(RS_ORDER[i - 1])
        if i > 2 and EARLY:
            project(RS_ORDER[i - 3])
    if not EARLY:
        wo_group.finish()
    wd_group.spread()
    heads_x.relay(0)
    for k in RS_ORDER[5 if EARLY else 0 :]:
        project(k)

    rows = ag[0]
    residual = total[...]
    sums = jnp.sum(residual * residual, axis=-1, keepdims=True)
    square[...] = jnp.broadcast_to(sums, (ZB, 128))
    square_box = Inbox(send, square_sem, home)
    for o in XO:
        square_box.push(square, square_in.at[o - 1], (o - 1,), net.xdev(o))
    for o in XO:
        square_box.wait(square_in.at[o - 1], (o - 1,))
        sums = sums + square_in[o - 1][:, 0:1]
    mean_sq = sums * (1.0 / D)
    scaled = total[...] * lax.rsqrt(mean_sq + 1e-06) * gain[:, xcols(x)].astype(F32)
    rows[z, x] = scaled.astype(BF16)

    for copy in weights:
        copy.wait()

    def inner_block(k, q, h):
        part = (slice(0, 80), slice(80, 2 * ZB + RB))[h] if h is not None else slice(0, 2 * ZB + RB)
        return inner.at[net.zc(k), q, part]

    inner_x = AlongX(net, send, inner_block, inner_sem, TREE_I)
    fed = []
    lane = lax.broadcasted_iota(jnp.int32, (RB, FR * FREP), 1) // FR

    def feed(k):
        c = net.zc(k)
        chunk = jnp.concatenate([rows[c, q] for q in range(NX)], axis=1)
        dims = (((1,), (1,)), ((), ()))
        gate = lax.dot_general(chunk, wg[...], dims, preferred_element_type=F32)
        up = lax.dot_general(chunk, wu[...], dims, preferred_element_type=F32)
        act = gate / (1.0 + jnp.exp(-gate)) * up
        for j in range(2):
            inner[c, x, j * ZB : (j + 1) * ZB] = act[:, j * 128 : (j + 1) * 128].astype(BF16)
        rest = act[:, FM:FK]
        packed = rest[0:RB]
        for q in range(1, FREP):
            packed = jnp.where(lane == q, rest[q * RB : (q + 1) * RB], packed)
        inner[c, x, 2 * ZB : 2 * ZB + RB] = packed.astype(BF16)
        inner_x.push(k)
        if fed:
            inner_x.relay(fed[-1])
        fed.append(k)

    def between(stage):
        if stage == 0:
            wd_group.pass_on()
            return
        wd_group.finish()
        for q in range(NX):
            for g, low, count, to in (
                (0, 0, 48, 0),
                (1, 0, 48, 48),
                (2, 32, 16, 96),
                (3, 0, 48, 112),
                (4, 32, 16, 160),
                (5, 0, 48, 176),
                (6, 32, 16, 224),
                (7, 0, 16, 240),
            ):
                wd[q * FM + to : q * FM + to + count] = wd_in[q, g, low : low + count]
            for j in range(FREP):
                to = NX * FM + (q * FREP + j) * FR
                wd[to : to + FR] = wd_in[q, 7, 16 : 16 + FR]

    all_gather(net, send, feed, between, *ag)

    far_box = Inbox(send, far_sem, home)
    group = lax.broadcasted_iota(jnp.int32, (ZB, FR * FREP), 1) // FR
    mine = group == lax.broadcasted_iota(jnp.int32, (ZB, FR * FREP), 0) // RB
    for k in (-3, 3, 4, -2, 2, -1, 1, 0) if FAR else RS_ORDER:
        c = net.zc(k)
        inner_x.finish(k)
        columns = []
        for q in range(NX):
            columns += [inner[c, q, 0:ZB], inner[c, q, ZB : 2 * ZB]]
        for q in range(NX):
            rest = jnp.concatenate([inner[c, q, 2 * ZB : 2 * ZB + RB]] * FREP, axis=0)
            columns.append(jnp.where(mine, rest, jnp.zeros_like(rest)))
        term = jnp.dot(jnp.concatenate(columns, axis=1), wd[...], preferred_element_type=F32)
        if k == 4 and FAR:
            far[...] = term.astype(BF16)
            far_box.push(far, far_in, (), net.zdev(4))
            continue
        if k:
            sum_ffn.step(k, term, chained=not FAR)
            continue
        if FAR:
            far_box.wait(far_in, ())
            term = term + far_in[...].astype(F32)
        for h in range(2):
            value = total[half(h)] + (term[half(h)] + sum_ffn.last(h))
            result[2 * h : 2 * h + 2] = value.astype(BF16).reshape(2, RB, DX)

    result_box = Inbox(send, result_sem, home)
    for o in XO:
        result_box.push(result.at[net.xc(o)], result_in.at[x], (o - 1,), net.xdev(o))
    result_in[x] = result[x]
    for o in XO:
        result_box.wait(result_in.at[net.xc(-o)], (o - 1,))
    live = lax.broadcasted_iota(jnp.int32, (RB, DX), 0) < counts[0]
    for q in range(NX):
        value = result_in[q]
        out[:, xcols(q)] = jnp.where(live, value, jnp.zeros_like(value))
    send.finish()


def per_device(
    query,
    cache,
    new_latent,
    lengths,
    counts,
    hidden_in,
    value_up,
    out_proj,
    norm_gain,
    w_gate,
    w_up,
    w_down,
):
    cache = cache.transpose(0, 2, 1)
    w_gate, w_up = w_gate.T, w_up.T
    vmem = pl.BlockSpec(memory_space=pltpu.VMEM)
    smem = pl.BlockSpec(memory_space=pltpu.SMEM)
    hbm = pl.BlockSpec(memory_space=pl.ANY)
    dma = pltpu.SemaphoreType.DMA
    return pl.pallas_call(
        layer_kernel,
        out_shape=jax.ShapeDtypeStruct((RB, D), BF16),
        in_specs=[hbm, hbm, vmem, smem, hbm, vmem, vmem, smem, hbm, hbm, hbm, hbm],
        out_specs=vmem,
        scratch_shapes=[
            pltpu.VMEM(query.shape, BF16),
            pltpu.VMEM(cache.shape, BF16),
            pltpu.VMEM((NZ, 2, KVL, VHD), BF16),
            pltpu.VMEM((NX, RB, 16, KVL), BF16),
            pltpu.VMEM((3, RB, 16, KVL), BF16),
            pltpu.VMEM((16, NX, RB, KVL), BF16),
            pltpu.VMEM((NZ, ZB, 2 * VHD), BF16),
            pltpu.VMEM((NZ, NX, ZB, 2 * VHD), BF16),
            dma((GROUPS,)),
            dma((GROUPS,)),
            dma((2, 3, GROUPS)),
            dma((2, 7)),
            ALONG_X_SEM,
            dma((2, 2, 4)),
            dma((2, 2, 4)),
            pltpu.VMEM((32, D), BF16),
            pltpu.VMEM((NX, 8, 32, DX), BF16),
            pltpu.VMEM((48, D), BF16),
            pltpu.VMEM((NX, 8, 48, DX), BF16),
            pltpu.VMEM((NX * FK, DX), BF16),
            pltpu.VMEM((FK, D), BF16),
            pltpu.VMEM((FK, D), BF16),
            dma((3,)),
            dma((2, FREP)),
            pltpu.VMEM((NZ, NX, 2 * ZB + RB, 128), BF16),
            ALONG_X_SEM,
            pltpu.VMEM((NX, RB, DX), BF16),
            dma((2, 3)),
            pltpu.VMEM((ZB, 128), F32),
            pltpu.VMEM((3, ZB, 128), F32),
            dma((2, 3)),
            pltpu.VMEM((ZB, DX), F32),
            pltpu.VMEM((NX, RB, DX), BF16),
            pltpu.VMEM((NX, RB, DX), BF16),
            dma((2, 3)),
            pltpu.VMEM((ZB, DX), BF16),
            pltpu.VMEM((ZB, DX), BF16),
            dma((2,)),
            *SUM_SCRATCH,
            *SUM_SCRATCH,
            *REGROUP_SEMS,
            *REGROUP_SEMS,
            *AG_SCRATCH,
        ],
        compiler_params=pltpu.CompilerParams(
            collective_id=1, has_side_effects=True, vmem_limit_bytes=60 << 20
        ),
        name="layer",
    )(
        query,
        cache,
        new_latent,
        lengths,
        value_up,
        hidden_in,
        norm_gain.reshape(1, D),
        counts,
        out_proj,
        w_gate,
        w_up,
        w_down,
    )


def solution(mesh):
    return jax.shard_map(
        per_device,
        mesh=mesh,
        in_specs=(
            P(("grp", "dp"), None, None),
            P(("grp", "dp"), None, None),
            P(("grp", "dp"), None),
            P(("grp", "dp")),
            P(("grp", "dp")),
            P(("grp", "dp"), None),
            P("dp", None, None),
            P("dp", None),
            P(),
            P(None, "dp"),
            P(None, "dp"),
            P("dp", None),
        ),
        out_specs=P(("grp", "dp"), None),
        check_vma=False,
    )
```

time: 149 us -> 126 us (0.85)
  Pallas kernels: 145 us -> 122 us
    pallas_call x1, Pallas kernels: 145 us -> 122 us  [per_device(): pl.pallas_call(layer_kernel, out_shape=jax.ShapeDtypeStruct((RB, D), BF16...]
where the time goes in v3:
time: 126 us; the launch traced here: 125 us
  Pallas kernels  122 us (97%)
  local copies, waits for them, and re-layouts  2.86 us (2%)
    pallas_call x1, Pallas kernels, per_device(): pl.pallas_call(layer_kernel, out_shape=jax.ShapeDtypeStruct((RB, D), BF16...  122 us

profile of v3, /device:TPU:8, one launch (start us, length us, event | category | flops | bytes accessed | tf_op | source)
XLA Modules:
  0.0 125.1 jit_solution(8583664046890675756)
XLA Ops:
  0.7 1.3 %reshape.3.gain = bf16[1,3584]{1,0:T(2,128)(2,1)} reshape(bf16[3584]{0:T(1024)(128)(2,1)} %param.20) | data formatting | bytes 14336 | tf_op jit(solution)/shard_map/reshape | solution.py:795
  2.0 121.6 %layer.1 = bf16[16,3584]{1,0:T(8,128)(2,1)} custom-call(bf16[16,64,576]{2,1,0:T(8,128)(2,1)} %query_hbm.1, bf16[16,576,256]{2,1,0:T(8,128)(2,1)} %bitcast.3, bf16[16,576]{1,0:T(8,128)(2,1)} %new_latent.1, s32[16]{0:T(128)} %lengths.1, bf16[2,512,128]{2,1,0:T(8,128)(2,1)} %vu_hbm.1, bf16[16,3584]{1,0:T(8,128)(2,1)} %hidden.1, bf16[1,3584]{1,0:T(2,128)(2,1)} %reshape.3.gain, ...), custom_call_target="tpu_custom_call" | custom-call | tf_op jit(solution)/shard_map/layer/pallas_call | solution.py:734
  123.6 1.6 %copy.15 = bf16[16,3584]{1,0:T(8,128)(2,1)} copy(bf16[16,3584]{1,0:T(8,128)(2,1)} %layer.1) | data formatting | bytes 229376

commit v4 on v3

--- a/solution.py
+++ b/solution.py
@@ -23,9 +23,6 @@
 FK = FM + FR * FREP
 CA = 384
 PLUS, MINUS = 0, 1
-TREE_A, TREE_H, TREE_I = False, False, False
-EARLY = False
-FAR = True
 STEP = (1, -1)
 XO = (1, 3, 2)
 RS_ORDER = (4, -3, 3, -2, 2, -1, 1, 0)
@@ -114,44 +111,21 @@
 
 
 class AlongX:
-    def __init__(self, net, send, block, sem, tree):
+    def __init__(self, net, send, block, sem):
         self.net, self.block = net, block
         self.box = Inbox(send, sem, net.zdev(0))
-        self.tree = tree
-
-    def relayed(self, k):
-        return self.tree and k != 4
 
     def push(self, k):
-        i = RS_ORDER.index(k)
-        ref = self.block(k, self.net.x, None)
-        for d in (PLUS, MINUS):
-            self.box.push(ref, ref, (i, d, 0), self.net.xdev(STEP[d]))
-        if not self.relayed(k):
-            self.box.push(ref, ref, (i, 0, 1), self.net.xdev(2))
-
-    def relay(self, k, last=False):
-        if not (self.relayed(k) or last):
-            return
-        i = RS_ORDER.index(k)
-        for d in (PLUS, MINUS):
-            come = self.net.xc(-STEP[d])
-            self.box.wait(self.block(k, come, None), (i, d, 0))
-            if not last:
-                ref = self.block(k, come, d)
-                self.box.push(ref, ref, (i, d, 1), self.net.xdev(STEP[d]))
+        ref = self.block(k, self.net.x)
+        for o in XO:
+            self.box.push(ref, ref, (o - 1, RS_ORDER.index(k)), self.net.xdev(o))
 
     def finish(self, k):
-        i = RS_ORDER.index(k)
-        if not self.relayed(k):
-            self.relay(k, True)
-            self.box.wait(self.block(k, self.net.xc(2), None), (i, 0, 1))
-            return
-        for d in (PLUS, MINUS):
-            self.box.wait(self.block(k, self.net.xc(2), d), (i, d, 1))
-
-
-ALONG_X_SEM = pltpu.SemaphoreType.DMA((2, NZ, 2, 2))
+        for o in XO:
+            self.box.wait(self.block(k, self.net.xc(-o)), (o - 1, RS_ORDER.index(k)))
+
+
+ALONG_X_SEM = pltpu.SemaphoreType.DMA((2, 3, NZ))
 
 
 class Regroup:
@@ -248,10 +222,10 @@
     home = net.zdev(0)
     az, bz, bx = (Inbox(send, sem, home) for sem in (az_sem, bz_sem, bx_sem))
 
-    def a_block(k, q, h):
-        return rows.at[net.zc(k), q, slice(0, ZB) if h is None else half(h), 0:CA]
-
-    ax = AlongX(net, send, a_block, ax_sem, TREE_A)
+    def a_block(k, q):
+        return rows.at[net.zc(k), q, :, 0:CA]
+
+    ax = AlongX(net, send, a_block, ax_sem)
 
     def a_ref(k, hops, d):
         return rows.at[net.zc(k), x, slice(0, ZB) if hops < 4 else half(d), 0:CA]
@@ -283,9 +257,10 @@
             if hops < 3 or (hops == 3 and far):
                 b_send(hops + 1, d, h)
 
-    def finish(k):
-        ax.finish(k)
-        use(k)
+    def finish(*ks):
+        for k in ks:
+            ax.finish(k)
+        use(ks)
 
     for d in (PLUS, MINUS):
         a_send(1, d)
@@ -299,31 +274,20 @@
     for far in (True, False):
         for d in (PLUS, MINUS):
             b_send(1, d, d if far else 1 - d)
-    ax.relay(0)
     step_a(2)
-    ax.relay(-1)
-    ax.relay(1)
     finish(0)
     step_b(1, True)
     step_a(3)
-    ax.relay(-2)
-    ax.relay(2)
     step_b(1, False)
     step_a(4)
-    finish(-1)
-    ax.relay(-3)
-    ax.relay(3)
-    finish(1)
+    finish(-1, 1)
     step_b(2, True)
-    ax.relay(4)
     step_b(2, False)
-    finish(-2)
+    finish(-2, 2)
     step_b(3, True)
-    finish(2)
     step_b(3, False)
     between(0)
-    finish(-3)
-    finish(3)
+    finish(-3, 3)
     step_b(4, True)
     between(1)
     finish(4)
@@ -455,6 +419,7 @@
     far,
     far_in,
     far_sem,
+    gain_row,
     *scratch,
 ):
     net = Net()
@@ -506,6 +471,7 @@
 
     begin([*loads[0], own_vu, own_wo, *loads[1]])
 
+    gain_row[...] = gain[...].astype(F32).reshape(1, D)
     value_up = ValueUp(net, send, vu, vz_sem, vcore_sem)
     order = order_matrix(
         64, lambda i: ((i & 15) >> 1) * 8 + (i >> 4) * 2 + (i & 1)
@@ -568,10 +534,10 @@
         if k:
             heads_box.push(heads_out.at[c], heads.at[z, x], (i,), net.zdev(k))
 
-    def heads_block(k, q, h):
-        return heads.at[net.zc(k), q, slice(0, ZB) if h is None else half(h)]
-
-    heads_x = AlongX(net, send, heads_block, heads_x_sem, TREE_H)
+    def heads_block(k, q):
+        return heads.at[net.zc(k), q]
+
+    heads_x = AlongX(net, send, heads_block, heads_x_sem)
 
     def project(k):
         c = net.zc(k)
@@ -591,51 +557,51 @@
         if k:
             heads_box.wait(heads.at[net.zc(k), x], (z_others.index(-k if k < 4 else 4),))
         heads_x.push(k)
-        if i == 2 and EARLY:
-            wo_group.finish()
-        if i:
-            heads_x.relay(RS_ORDER[i - 1])
-        if i > 2 and EARLY:
-            project(RS_ORDER[i - 3])
-    if not EARLY:
-        wo_group.finish()
+    wo_group.finish()
     wd_group.spread()
-    heads_x.relay(0)
-    for k in RS_ORDER[5 if EARLY else 0 :]:
+    for k in RS_ORDER:
         project(k)
 
     rows = ag[0]
     residual = total[...]
     sums = jnp.sum(residual * residual, axis=-1, keepdims=True)
-    square[...] = jnp.broadcast_to(sums, (ZB, 128))
+    lane = lax.broadcasted_iota(jnp.int32, (RB, FR * FREP), 1) // FR
+    packed = jnp.broadcast_to(sums[0:RB], (RB, 128))
+    for q in range(1, FREP):
+        packed = jnp.where(lane == q, sums[q * RB : (q + 1) * RB], packed)
+    square[...] = packed
     square_box = Inbox(send, square_sem, home)
     for o in XO:
         square_box.push(square, square_in.at[o - 1], (o - 1,), net.xdev(o))
     for o in XO:
         square_box.wait(square_in.at[o - 1], (o - 1,))
-        sums = sums + square_in[o - 1][:, 0:1]
+        packed = packed + square_in[o - 1]
+    sums = jnp.concatenate([packed[:, q * FR : q * FR + 1] for q in range(FREP)], axis=0)
     mean_sq = sums * (1.0 / D)
-    scaled = total[...] * lax.rsqrt(mean_sq + 1e-06) * gain[:, xcols(x)].astype(F32)
+    scaled = total[...] * lax.rsqrt(mean_sq + 1e-06) * gain_row[:, xcols(x)]
     rows[z, x] = scaled.astype(BF16)
 
     for copy in weights:
         copy.wait()
 
-    def inner_block(k, q, h):
-        part = (slice(0, 80), slice(80, 2 * ZB + RB))[h] if h is not None else slice(0, 2 * ZB + RB)
-        return inner.at[net.zc(k), q, part]
-
-    inner_x = AlongX(net, send, inner_block, inner_sem, TREE_I)
-    fed = []
-    lane = lax.broadcasted_iota(jnp.int32, (RB, FR * FREP), 1) // FR
-
-    def feed(k):
-        c = net.zc(k)
-        chunk = jnp.concatenate([rows[c, q] for q in range(NX)], axis=1)
+    def inner_block(k, q):
+        return inner.at[net.zc(k), q]
+
+    inner_x = AlongX(net, send, inner_block, inner_sem)
+
+    def feed(ks):
+        chunk = jnp.concatenate(
+            [jnp.concatenate([rows[net.zc(k), q] for q in range(NX)], axis=1) for k in ks], axis=0
+        )
         dims = (((1,), (1,)), ((), ()))
         gate = lax.dot_general(chunk, wg[...], dims, preferred_element_type=F32)
         up = lax.dot_general(chunk, wu[...], dims, preferred_element_type=F32)
         act = gate / (1.0 + jnp.exp(-gate)) * up
+        for i, k in enumerate(ks):
+            store(k, act[i * ZB : (i + 1) * ZB])
+
+    def store(k, act):
+        c = net.zc(k)
         for j in range(2):
             inner[c, x, j * ZB : (j + 1) * ZB] = act[:, j * 128 : (j + 1) * 128].astype(BF16)
         rest = act[:, FM:FK]
@@ -644,9 +610,6 @@
             packed = jnp.where(lane == q, rest[q * RB : (q + 1) * RB], packed)
         inner[c, x, 2 * ZB : 2 * ZB + RB] = packed.astype(BF16)
         inner_x.push(k)
-        if fed:
-            inner_x.relay(fed[-1])
-        fed.append(k)
 
     def between(stage):
         if stage == 0:
@@ -674,7 +637,7 @@
     far_box = Inbox(send, far_sem, home)
     group = lax.broadcasted_iota(jnp.int32, (ZB, FR * FREP), 1) // FR
     mine = group == lax.broadcasted_iota(jnp.int32, (ZB, FR * FREP), 0) // RB
-    for k in (-3, 3, 4, -2, 2, -1, 1, 0) if FAR else RS_ORDER:
+    for k in (-3, 3, 4, -2, 2, -1, 1, 0):
         c = net.zc(k)
         inner_x.finish(k)
         columns = []
@@ -684,16 +647,15 @@
             rest = jnp.concatenate([inner[c, q, 2 * ZB : 2 * ZB + RB]] * FREP, axis=0)
             columns.append(jnp.where(mine, rest, jnp.zeros_like(rest)))
         term = jnp.dot(jnp.concatenate(columns, axis=1), wd[...], preferred_element_type=F32)
-        if k == 4 and FAR:
+        if k == 4:
             far[...] = term.astype(BF16)
             far_box.push(far, far_in, (), net.zdev(4))
             continue
         if k:
-            sum_ffn.step(k, term, chained=not FAR)
+            sum_ffn.step(k, term, chained=False)
             continue
-        if FAR:
-            far_box.wait(far_in, ())
-            term = term + far_in[...].astype(F32)
+        far_box.wait(far_in, ())
+        term = term + far_in[...].astype(F32)
         for h in range(2):
             value = total[half(h)] + (term[half(h)] + sum_ffn.last(h))
             result[2 * h : 2 * h + 2] = value.astype(BF16).reshape(2, RB, DX)
@@ -765,8 +727,8 @@
             ALONG_X_SEM,
             pltpu.VMEM((NX, RB, DX), BF16),
             dma((2, 3)),
-            pltpu.VMEM((ZB, 128), F32),
-            pltpu.VMEM((3, ZB, 128), F32),
+            pltpu.VMEM((RB, 128), F32),
+            pltpu.VMEM((3, RB, 128), F32),
             dma((2, 3)),
             pltpu.VMEM((ZB, DX), F32),
             pltpu.VMEM((NX, RB, DX), BF16),
@@ -775,6 +737,7 @@
             pltpu.VMEM((ZB, DX), BF16),
             pltpu.VMEM((ZB, DX), BF16),
             dma((2,)),
+            pltpu.VMEM((1, D), F32),
             *SUM_SCRATCH,
             *SUM_SCRATCH,
             *REGROUP_SEMS,
@@ -792,7 +755,7 @@
         lengths,
         value_up,
         hidden_in,
-        norm_gain.reshape(1, D),
+        norm_gain,
         counts,
         out_proj,
         w_gate,

time: 126 us -> 121 us (0.960)
  Pallas kernels: 122 us -> 119 us
  local copies, waits for them, and re-layouts: 2.86 us -> 1.55 us
    pallas_call x1, Pallas kernels: 122 us -> 119 us  [per_device(): pl.pallas_call(layer_kernel, out_shape=jax.ShapeDtypeStruct((RB, D), BF16...]
    reshape x1 -> x0, local copies, waits for them, and re-layouts: 1.31 us -> none  [per_device(): norm_gain.reshape(1, D)]
where the time goes in v4:
time: 121 us
  Pallas kernels  119 us (98%)
  local copies, waits for them, and re-layouts  1.55 us (1%)
    pallas_call x1, Pallas kernels, per_device(): pl.pallas_call(layer_kernel, out_shape=jax.ShapeDtypeStruct((RB, D), BF16...  119 us

profile of v4, /device:TPU:8, one launch (start us, length us, event | category | flops | bytes accessed | tf_op | source)
XLA Modules:
  0.0 120.7 jit_solution(1482420130461350603)
XLA Ops:
  0.7 118.5 %layer.1 = bf16[16,3584]{1,0:T(8,128)(2,1)} custom-call(bf16[16,64,576]{2,1,0:T(8,128)(2,1)} %query_hbm.1, bf16[16,576,256]{2,1,0:T(8,128)(2,1)} %bitcast.3, bf16[16,576]{1,0:T(8,128)(2,1)} %new_latent.1, s32[16]{0:T(128)} %lengths.1, bf16[2,512,128]{2,1,0:T(8,128)(2,1)} %vu_hbm.1, bf16[16,3584]{1,0:T(8,128)(2,1)} %hidden.1, bf16[3584]{0:T(1024)(128)(2,1)} %gain.1, ...), custom_call_target="tpu_custom_call" | custom-call | tf_op jit(solution)/shard_map/layer/pallas_call | solution.py:696
  119.2 1.6 %copy.15 = bf16[16,3584]{1,0:T(8,128)(2,1)} copy(bf16[16,3584]{1,0:T(8,128)(2,1)} %layer.1) | data formatting | bytes 229376

commit v5 on v4

--- a/solution.py
+++ b/solution.py
@@ -539,11 +539,17 @@
 
     heads_x = AlongX(net, send, heads_block, heads_x_sem)
 
-    def project(k):
-        c = net.zc(k)
-        heads_x.finish(k)
-        rows = jnp.concatenate([heads[c, q] for q in range(NX)], axis=1)
-        term = jnp.dot(rows, wo[...].reshape(NX * 256, DX), preferred_element_type=F32)
+    def project(ks):
+        for k in ks:
+            heads_x.finish(k)
+        rows = jnp.concatenate(
+            [jnp.concatenate([heads[net.zc(k), q] for q in range(NX)], axis=1) for k in ks], axis=0
+        )
+        terms = jnp.dot(rows, wo[...].reshape(NX * 256, DX), preferred_element_type=F32)
+        for i, k in enumerate(ks):
+            add_heads(k, terms[i * ZB : (i + 1) * ZB])
+
+    def add_heads(k, term):
         if k:
             sum_heads.step(k, term)
             return
@@ -559,8 +565,8 @@
         heads_x.push(k)
     wo_group.finish()
     wd_group.spread()
-    for k in RS_ORDER:
-        project(k)
+    for ks in ((4,), (-3, 3), (-2, 2), (-1, 1), (0,)):
+        project(ks)
 
     rows = ag[0]
     residual = total[...]
@@ -637,28 +643,38 @@
     far_box = Inbox(send, far_sem, home)
     group = lax.broadcasted_iota(jnp.int32, (ZB, FR * FREP), 1) // FR
     mine = group == lax.broadcasted_iota(jnp.int32, (ZB, FR * FREP), 0) // RB
-    for k in (-3, 3, 4, -2, 2, -1, 1, 0):
+
+    def inner_rows(k):
         c = net.zc(k)
-        inner_x.finish(k)
         columns = []
         for q in range(NX):
             columns += [inner[c, q, 0:ZB], inner[c, q, ZB : 2 * ZB]]
         for q in range(NX):
             rest = jnp.concatenate([inner[c, q, 2 * ZB : 2 * ZB + RB]] * FREP, axis=0)
             columns.append(jnp.where(mine, rest, jnp.zeros_like(rest)))
-        term = jnp.dot(jnp.concatenate(columns, axis=1), wd[...], preferred_element_type=F32)
+        return jnp.concatenate(columns, axis=1)
+
+    def add_ffn(k, term):
         if k == 4:
             far[...] = term.astype(BF16)
             far_box.push(far, far_in, (), net.zdev(4))
-            continue
+            return
         if k:
             sum_ffn.step(k, term, chained=False)
-            continue
+            return
         far_box.wait(far_in, ())
         term = term + far_in[...].astype(F32)
         for h in range(2):
             value = total[half(h)] + (term[half(h)] + sum_ffn.last(h))
             result[2 * h : 2 * h + 2] = value.astype(BF16).reshape(2, RB, DX)
+
+    for ks in ((-3, 3), (4,), (-2, 2), (-1, 1), (0,)):
+        for k in ks:
+            inner_x.finish(k)
+        rows_in = jnp.concatenate([inner_rows(k) for k in ks], axis=0)
+        terms = jnp.dot(rows_in, wd[...], preferred_element_type=F32)
+        for i, k in enumerate(ks):
+            add_ffn(k, terms[i * ZB : (i + 1) * ZB])
 
     result_box = Inbox(send, result_sem, home)
     for o in XO:

time: 121 us -> 121 us (level)
  no operation moved by 1% of the time
where the time goes in v5:
time: 121 us
  Pallas kernels  119 us (98%)
  local copies, waits for them, and re-layouts  1.55 us (1%)
    pallas_call x1, Pallas kernels, per_device(): pl.pallas_call(layer_kernel, out_shape=jax.ShapeDtypeStruct((RB, D), BF16...  119 us

profile of v5, /device:TPU:8, one launch (start us, length us, event | category | flops | bytes accessed | tf_op | source)
XLA Modules:
  0.0 120.8 jit_solution(14619963200793418861)
XLA Ops:
  0.7 118.6 %layer.1 = bf16[16,3584]{1,0:T(8,128)(2,1)} custom-call(bf16[16,64,576]{2,1,0:T(8,128)(2,1)} %query_hbm.1, bf16[16,576,256]{2,1,0:T(8,128)(2,1)} %bitcast.3, bf16[16,576]{1,0:T(8,128)(2,1)} %new_latent.1, s32[16]{0:T(128)} %lengths.1, bf16[2,512,128]{2,1,0:T(8,128)(2,1)} %vu_hbm.1, bf16[16,3584]{1,0:T(8,128)(2,1)} %hidden.1, bf16[3584]{0:T(1024)(128)(2,1)} %gain.1, ...), custom_call_target="tpu_custom_call" | custom-call | tf_op jit(solution)/shard_map/layer/pallas_call | solution.py:712
  119.3 1.6 %copy.15 = bf16[16,3584]{1,0:T(8,128)(2,1)} copy(bf16[16,3584]{1,0:T(8,128)(2,1)} %layer.1) | data formatting | bytes 229376
